TPU v7x, 32 devices: a whole 2x2x4 slice. The times are simulated.
32 devices in a mesh: dp: 16 (over z, y, x), rows: 2 (over core).
Axes of the slice: x: 2, y: 2, z: 4, core: 2. Of those that a mesh axis runs over, the one named last changes fastest.
Arguments:
- glob_in: bfloat16 [16, 28, 28, 1492], P('dp', 'rows'), may hold values from -6 to 6
- small_in: bfloat16 [80, 12, 12, 1492], P('dp', 'rows'), may hold values from -6 to 6
- small_count: int32 [16], P('dp'), may hold values from 1 to 5, as said below
- kernel_in: bfloat16 [1492, 1492], P(None, 'rows'), may hold values from -0.15625 to 0.15625
- kernel_mid: bfloat16 [3, 3, 373, 1492], P(None, None, None, 'rows'), may hold values from -0.109375 to 0.109375
- kernel_out: bfloat16 [1492, 1492], P(None, 'rows'), may hold values from -0.15625 to 0.15625
- squeeze_weight: bfloat16 [1492, 373], P('rows'), may hold values from -0.3125 to 0.3125
- squeeze_bias: bfloat16 [373], replicated, may hold values from -3 to 3
- excite_weight: bfloat16 [373, 1492], P(None, 'rows'), may hold values from -0.625 to 0.625
- excite_bias: bfloat16 [1492], P('rows'), may hold values from -3 to 3
- gain_first: bfloat16 [1492], P('rows'), may hold values from 0.099609375 to 1.8984375
- shift_first: bfloat16 [1492], P('rows'), may hold values from -3 to 3
- gain_second: bfloat16 [1492], P('rows'), may hold values from 0.099609375 to 1.8984375
- shift_second: bfloat16 [1492], P('rows'), may hold values from -3 to 3
- gain_third: bfloat16 [1492], P('rows'), may hold values from 0.099609375 to 1.8984375
- shift_third: bfloat16 [1492], P('rows'), may hold values from -3 to 3
- glob_cotangent: bfloat16 [16, 28, 28, 1492], P('dp', 'rows'), may hold values from -6 to 6
- small_cotangent: bfloat16 [80, 12, 12, 1492], P('dp', 'rows'), may hold values from -6 to 6
Outputs:
- glob_out: float32 [16, 28, 28, 1492], P('dp', 'rows')
- small_out: float32 [80, 12, 12, 1492], P('dp', 'rows')
- glob_grad: float32 [16, 28, 28, 1492], P('dp', 'rows')
- small_grad: float32 [80, 12, 12, 1492], P('dp', 'rows')
- grad_kernel_in: float32 [1492, 1492], P(None, 'rows')
- grad_kernel_mid: float32 [3, 3, 373, 1492], P(None, None, None, 'rows')
- grad_kernel_out: float32 [1492, 1492], P(None, 'rows')
- grad_squeeze_weight: float32 [1492, 373], P('rows')
- grad_squeeze_bias: float32 [373], replicated
- grad_excite_weight: float32 [373, 1492], P(None, 'rows')
- grad_excite_bias: float32 [1492], P('rows')
- grad_gain_first: float32 [1492], P('rows')
- grad_shift_first: float32 [1492], P('rows')
- grad_gain_second: float32 [1492], P('rows')
- grad_shift_second: float32 [1492], P('rows')
- grad_gain_third: float32 [1492], P('rows')
- grad_shift_third: float32 [1492], P('rows')
Inputs may be any that keep to these rules, and one draw needn't show every extreme that they name: Block b's live small crops are its first small_count[b] slots; some block uses all 5.
All inputs are finite; a program needn't handle non-finite values.
Results may differ from a plain program's by a relative error of at most 0.017.
Values may be sent and summed in bfloat16 or wider, within the bound.
A program may use at most 384 MiB of HBM per device.

v0:
```python
import jax
import jax.numpy as jnp
from jax import lax
from jax.sharding import PartitionSpec as P

EPSILON = 1e-05
HIGHEST = lax.Precision.HIGHEST


def extended(block, sides, width):
    for axis, dim in sides:
        count = lax.axis_size(axis)
        forward = [(i, i + 1) for i in range(count - 1)]
        backward = [(target, source) for source, target in forward]
        low = lax.ppermute(
            lax.slice_in_dim(block, block.shape[dim] - width, None, axis=dim), axis, forward
        )
        high = lax.ppermute(lax.slice_in_dim(block, 0, width, axis=dim), axis, backward)
        block = jnp.concatenate([low, block, high], axis=dim)
    return block


def silu_slope(values):
    sigma = jax.nn.sigmoid(values)
    return sigma * (1.0 + values * (1.0 - sigma))


def widen(maps):
    return jnp.pad(maps, ((0, 0), (0, 0), (1, 1), (0, 0)))


def rim_forward(maps):
    return widen(extended(maps, (("rows", 1),), 1))


def rim_backward(maps):
    return widen(extended(maps, (("rows", 1),), 1))


def tap_window(padded, row_start, col_start, height, breadth, groups):
    number = padded.shape[0]
    channels = padded.shape[3]
    window = padded[:, row_start : row_start + height, col_start : col_start + breadth]
    return window.reshape(number, height, breadth, groups, channels // groups)


def group_conv(padded, kernel, groups):
    number = padded.shape[0]
    height = padded.shape[1] - 2
    breadth = padded.shape[2] - 2
    channels = padded.shape[3]
    group_width = channels // groups
    running = jnp.zeros((number, height, breadth, groups, group_width), jnp.float32)
    for row_tap in range(3):
        for col_tap in range(3):
            window = tap_window(padded, row_tap, col_tap, height, breadth, groups)
            weights = kernel[row_tap, col_tap].reshape(group_width, groups, group_width)
            running = running + jnp.einsum(
                "mhwgc,cgo->mhwgo", window, weights, preferred_element_type=jnp.float32
            )
    return running.reshape(number * height * breadth, channels)


def group_conv_input(padded_grad, kernel, groups):
    number = padded_grad.shape[0]
    height = padded_grad.shape[1] - 2
    breadth = padded_grad.shape[2] - 2
    channels = padded_grad.shape[3]
    group_width = channels // groups
    running = jnp.zeros((number, height, breadth, groups, group_width), jnp.float32)
    for row_tap in range(3):
        for col_tap in range(3):
            window = tap_window(padded_grad, 2 - row_tap, 2 - col_tap, height, breadth, groups)
            weights = kernel[row_tap, col_tap].reshape(group_width, groups, group_width)
            running = running + jnp.einsum(
                "mhwgo,cgo->mhwgc", window, weights, preferred_element_type=jnp.float32
            )
    return running.reshape(number * height * breadth, channels)


def group_conv_kernel(padded, upstream, groups):
    number, height, breadth, channels = upstream.shape
    group_width = channels // groups
    grad_groups = upstream.reshape(number, height, breadth, groups, group_width)
    rows_out = []
    for row_tap in range(3):
        tap_terms = []
        for col_tap in range(3):
            window = tap_window(padded, row_tap, col_tap, height, breadth, groups)
            tap_piece = jnp.einsum(
                "mhwgc,mhwgo->cgo", window, grad_groups, preferred_element_type=jnp.float32
            )
            tap_terms.append(tap_piece.reshape(group_width, channels))
        rows_out.append(jnp.stack(tap_terms, 0))
    return jnp.stack(rows_out, 0)


def norm_forward(values, pixel_mask, local_count, norm_gain, norm_offset):
    first_sum, total_count = lax.psum(
        (jnp.sum(values * pixel_mask, 0), local_count), ("dp", "rows")
    )
    mean_value = first_sum / total_count
    centered = values - mean_value
    spread = lax.psum(jnp.sum(pixel_mask * centered * centered, 0), ("dp", "rows")) / total_count
    inverse = lax.rsqrt(spread + EPSILON)
    normed = centered * inverse
    return (normed * norm_gain + norm_offset, normed, inverse, total_count)


def norm_sums(upstream, normed):
    return lax.psum((jnp.sum(upstream, 0), jnp.sum(upstream * normed, 0)), ("dp", "rows"))


def norm_backward(
    upstream, normed, inverse, norm_gain, total_count, pixel_mask, shift_sum, gain_sum
):
    return (
        norm_gain
        * inverse
        * (upstream - shift_sum / total_count - normed * (gain_sum / total_count))
        * pixel_mask
    )


def halve_term(local_term):
    last_dim = local_term.shape[-1]
    return local_term.reshape(-1, 2, last_dim // 2).transpose(1, 0, 2).reshape(2, -1)


def spread_blocks(halves):
    blocks = lax.axis_size("dp")
    length = halves.shape[1]
    width = -(-length // blocks)
    padded = jnp.pad(halves, ((0, 0), (0, width * blocks - length)))
    return padded.reshape(2, blocks, width).transpose(1, 0, 2).reshape(2 * blocks, width)


def reduce_all(local_terms):
    pieces = [halve_term(local_item) for local_item in local_terms]
    joined = jnp.concatenate(pieces, 1)
    owned = lax.psum_scatter(spread_blocks(joined), ("dp", "rows"), scatter_dimension=0, tiled=True)
    gathered = (
        lax.all_gather(owned.astype(jnp.bfloat16), "dp", axis=0, tiled=True)
        .astype(owned.dtype)
        .reshape(-1)
    )
    results = []
    offset = 0
    for piece in pieces:
        part_width = piece.shape[1]
        results.append(gathered[offset : offset + part_width])
        offset = offset + part_width
    return results


def shard_shape(reduced_item, local_term):
    return reduced_item.reshape(local_term.shape[:-1] + (local_term.shape[-1] // 2,))


def per_device(
    glob_in,
    small_in,
    small_count,
    kernel_in,
    kernel_mid,
    kernel_out,
    squeeze_weight,
    squeeze_bias,
    excite_weight,
    excite_bias,
    gain_first,
    shift_first,
    gain_second,
    shift_second,
    gain_third,
    shift_third,
    glob_cotangent,
    small_cotangent,
):
    gathered = (
        lax.all_gather(kernel_in, "rows", axis=1, tiled=True),
        lax.all_gather(kernel_mid, "rows", axis=3, tiled=True),
        lax.all_gather(kernel_out, "rows", axis=1, tiled=True),
        lax.all_gather(squeeze_weight, "rows", axis=0, tiled=True),
        lax.all_gather(excite_weight, "rows", axis=1, tiled=True),
        lax.all_gather(excite_bias, "rows", axis=0, tiled=True),
        lax.all_gather(gain_first, "rows", axis=0, tiled=True),
        lax.all_gather(shift_first, "rows", axis=0, tiled=True),
        lax.all_gather(gain_second, "rows", axis=0, tiled=True),
        lax.all_gather(shift_second, "rows", axis=0, tiled=True),
        lax.all_gather(gain_third, "rows", axis=0, tiled=True),
        lax.all_gather(shift_third, "rows", axis=0, tiled=True),
    )
    matrix_in = gathered[0]
    matrix_mid = gathered[1]
    matrix_out = gathered[2]
    squeeze_matrix = gathered[3].astype(jnp.float32)
    squeeze_vector = squeeze_bias.astype(jnp.float32)
    excite_matrix = gathered[4].astype(jnp.float32)
    excite_vector = gathered[5].astype(jnp.float32)
    norm_gains = [
        gathered[6].astype(jnp.float32),
        gathered[8].astype(jnp.float32),
        gathered[10].astype(jnp.float32),
    ]
    norm_offsets = [
        gathered[7].astype(jnp.float32),
        gathered[9].astype(jnp.float32),
        gathered[11].astype(jnp.float32),
    ]
    channels = glob_in.shape[3]
    groups = channels // matrix_mid.shape[2]
    row_devices = lax.axis_size("rows")
    row_share = 1.0 / row_devices
    row_index = lax.axis_index("rows")
    glob_maps = glob_in.shape[0]
    glob_rows = glob_in.shape[1]
    glob_side = glob_in.shape[2]
    slot_total = small_in.shape[0]
    small_rows = small_in.shape[1]
    small_side = small_in.shape[2]
    glob_pixels = glob_maps * glob_rows * glob_side
    glob_area = float(glob_rows * row_devices * glob_side)
    small_area = float(small_rows * row_devices * small_side)
    crop_areas = jnp.concatenate(
        [
            jnp.full((glob_maps, 1), glob_area, jnp.float32),
            jnp.full((slot_total, 1), small_area, jnp.float32),
        ],
        0,
    )
    live_slots = (lax.iota(jnp.int32, slot_total) < small_count[0]).astype(jnp.float32)
    small_mask = jnp.broadcast_to(
        live_slots[:, None], (slot_total, small_rows * small_side)
    ).reshape(-1, 1)
    pixel_mask = jnp.concatenate([jnp.ones((glob_pixels, 1), jnp.float32), small_mask], 0)
    local_count = jnp.sum(pixel_mask)
    inputs = jnp.concatenate([glob_in.reshape(-1, channels), small_in.reshape(-1, channels)], 0)

    def glob_part(flat_rows):
        return flat_rows[:glob_pixels].reshape(glob_maps, glob_rows, glob_side, -1)

    def small_part(flat_rows):
        return flat_rows[glob_pixels:].reshape(slot_total, small_rows, small_side, -1)

    def crop_sums(flat_rows):
        return (
            jnp.sum(flat_rows[:glob_pixels].reshape(glob_maps, -1, channels), 1),
            jnp.sum(flat_rows[glob_pixels:].reshape(slot_total, -1, channels), 1),
        )

    def per_pixel(per_crop):
        leading = jnp.broadcast_to(
            per_crop[:glob_maps, None, :], (glob_maps, glob_rows * glob_side, channels)
        ).reshape(-1, channels)
        trailing = jnp.broadcast_to(
            per_crop[glob_maps:, None, :], (slot_total, small_rows * small_side, channels)
        ).reshape(-1, channels)
        return jnp.concatenate([leading, trailing], 0)

    def own_half(vector):
        half_len = vector.shape[0] // 2
        return lax.dynamic_slice_in_dim(vector, row_index * half_len, half_len)

    pre_one = jnp.dot(inputs, matrix_in, preferred_element_type=jnp.float32)
    norm_one, hat_one, inverse_one, count_one = norm_forward(
        pre_one, pixel_mask, local_count, norm_gains[0], norm_offsets[0]
    )
    act_one = jax.nn.silu(norm_one).astype(jnp.bfloat16)
    glob_padded = rim_forward(glob_part(act_one))
    small_padded = rim_forward(small_part(act_one))
    pre_two = jnp.concatenate(
        [group_conv(glob_padded, matrix_mid, groups), group_conv(small_padded, matrix_mid, groups)],
        0,
    )
    norm_two, hat_two, inverse_two, count_two = norm_forward(
        pre_two, pixel_mask, local_count, norm_gains[1], norm_offsets[1]
    )
    act_two = jax.nn.silu(norm_two)
    glob_sum, small_sum = crop_sums(act_two)
    glob_pool, small_pool = (
        lax.psum(glob_sum.astype(jnp.bfloat16), "rows").astype(jnp.float32),
        lax.psum(small_sum.astype(jnp.bfloat16), "rows").astype(jnp.float32),
    )
    pooled = jnp.concatenate([glob_pool, small_pool], 0) / crop_areas
    squeeze_pre = jnp.dot(pooled, squeeze_matrix, precision=HIGHEST) + squeeze_vector
    squeezed = jax.nn.silu(squeeze_pre)
    excite = jax.nn.sigmoid(jnp.dot(squeezed, excite_matrix, precision=HIGHEST) + excite_vector)
    excite_pixels = per_pixel(excite)
    act_three = (act_two * excite_pixels).astype(jnp.bfloat16)
    pre_three = jnp.dot(act_three, matrix_out, preferred_element_type=jnp.float32)
    norm_three, hat_three, inverse_three, count_three = norm_forward(
        pre_three, pixel_mask, local_count, norm_gains[2], norm_offsets[2]
    )
    summed = norm_three + inputs.astype(jnp.float32)
    result = pixel_mask * jax.nn.silu(summed)
    cotangent = jnp.concatenate(
        [glob_cotangent.reshape(-1, channels), small_cotangent.reshape(-1, channels)], 0
    ).astype(jnp.float32)
    early = []

    def record(local_term):
        early.append(local_term)

    grad_summed = cotangent * pixel_mask * silu_slope(summed)
    shift_three_sum, gain_three_sum = norm_sums(grad_summed, hat_three)
    grad_pre_three = norm_backward(
        grad_summed,
        hat_three,
        inverse_three,
        norm_gains[2],
        count_three,
        pixel_mask,
        shift_three_sum,
        gain_three_sum,
    ).astype(jnp.bfloat16)
    term_out = jnp.dot(act_three.T, grad_pre_three, preferred_element_type=jnp.float32)
    record(term_out)
    grad_act_three = jnp.dot(grad_pre_three, matrix_out.T, preferred_element_type=jnp.float32)
    glob_grad_sum, small_grad_sum = crop_sums(grad_act_three * act_two)
    glob_excite, small_excite = (
        lax.psum(glob_grad_sum.astype(jnp.bfloat16), "rows").astype(jnp.float32),
        lax.psum(small_grad_sum.astype(jnp.bfloat16), "rows").astype(jnp.float32),
    )
    grad_excite_pre = jnp.concatenate([glob_excite, small_excite], 0) * excite * (1.0 - excite)
    term_excite = row_share * jnp.dot(squeezed.T, grad_excite_pre, precision=HIGHEST)
    record(term_excite)
    grad_squeeze_pre = jnp.dot(grad_excite_pre, excite_matrix.T, precision=HIGHEST) * silu_slope(
        squeeze_pre
    )
    term_squeeze = row_share * jnp.dot(grad_squeeze_pre.T, pooled, precision=HIGHEST)
    record(term_squeeze)
    grad_pooled = jnp.dot(grad_squeeze_pre, squeeze_matrix.T, precision=HIGHEST) / crop_areas
    grad_act_two = grad_act_three * excite_pixels + per_pixel(grad_pooled)
    grad_norm_two = grad_act_two * silu_slope(norm_two)
    shift_two_sum, gain_two_sum, squeeze_bias_sum, excite_bias_sum = lax.psum(
        (
            jnp.sum(grad_norm_two, 0),
            jnp.sum(grad_norm_two * hat_two, 0),
            row_share * jnp.sum(grad_squeeze_pre, 0),
            row_share * jnp.sum(grad_excite_pre, 0),
        ),
        ("dp", "rows"),
    )
    grad_pre_two = norm_backward(
        grad_norm_two,
        hat_two,
        inverse_two,
        norm_gains[1],
        count_two,
        pixel_mask,
        shift_two_sum,
        gain_two_sum,
    ).astype(jnp.bfloat16)
    glob_upstream = glob_part(grad_pre_two)
    small_upstream = small_part(grad_pre_two)
    grad_act_one = jnp.concatenate(
        [
            group_conv_input(rim_backward(glob_upstream), matrix_mid, groups),
            group_conv_input(rim_backward(small_upstream), matrix_mid, groups),
        ],
        0,
    )
    term_mid = group_conv_kernel(glob_padded, glob_upstream, groups) + group_conv_kernel(
        small_padded, small_upstream, groups
    )
    record(term_mid)
    grad_norm_one = grad_act_one * silu_slope(norm_one)
    shift_one_sum, gain_one_sum = norm_sums(grad_norm_one, hat_one)
    grad_pre_one = norm_backward(
        grad_norm_one,
        hat_one,
        inverse_one,
        norm_gains[0],
        count_one,
        pixel_mask,
        shift_one_sum,
        gain_one_sum,
    ).astype(jnp.bfloat16)
    term_in = jnp.dot(inputs.T, grad_pre_one, preferred_element_type=jnp.float32)
    record(term_in)
    grad_inputs = grad_summed + jnp.dot(
        grad_pre_one, matrix_in.T, preferred_element_type=jnp.float32
    )
    local_terms = [term_out, term_excite, term_squeeze, term_mid, term_in]
    reduced = reduce_all(early)
    grad_out = shard_shape(reduced[0], local_terms[0])
    grad_excite = shard_shape(reduced[1], local_terms[1])
    grad_squeeze = shard_shape(reduced[2], local_terms[2]).T
    grad_mid = shard_shape(reduced[3], local_terms[3])
    grad_in = shard_shape(reduced[4], local_terms[4])
    return (
        glob_part(result),
        small_part(result),
        glob_part(grad_inputs),
        small_part(grad_inputs),
        grad_in,
        grad_mid,
        grad_out,
        grad_squeeze,
        squeeze_bias_sum,
        grad_excite,
        own_half(excite_bias_sum),
        own_half(gain_one_sum),
        own_half(shift_one_sum),
        own_half(gain_two_sum),
        own_half(shift_two_sum),
        own_half(gain_three_sum),
        own_half(shift_three_sum),
    )


def solution(mesh):
    return jax.shard_map(
        per_device,
        mesh=mesh,
        in_specs=(
            P("dp", "rows", None, None),
            P("dp", "rows", None, None),
            P("dp"),
            P(None, "rows"),
            P(None, None, None, "rows"),
            P(None, "rows"),
            P("rows", None),
            P(),
            P(None, "rows"),
            P("rows"),
            P("rows"),
            P("rows"),
            P("rows"),
            P("rows"),
            P("rows"),
            P("rows"),
            P("dp", "rows", None, None),
            P("dp", "rows", None, None),
        ),
        out_specs=(
            P("dp", "rows", None, None),
            P("dp", "rows", None, None),
            P("dp", "rows", None, None),
            P("dp", "rows", None, None),
            P(None, "rows"),
            P(None, None, None, "rows"),
            P(None, "rows"),
            P("rows", None),
            P(),
            P(None, "rows"),
            P("rows"),
            P("rows"),
            P("rows"),
            P("rows"),
            P("rows"),
            P("rows"),
            P("rows"),
        ),
        check_vma=False,
    )
```

profile of v0, /device:TPU:0, one launch (start us, length us, event | category | flops | bytes accessed | tf_op | source)
XLA Modules:
  0.0 3557.4 jit_solution(3136487286955122663)
XLA Ops:
  11.5 13.2 copy.393
  76.3 41.8 %all-reduce.18 = (f32[1492]{0:T(1024)S(1)}, f32[]{:T(128)}) all-reduce(f32[1492]{0:T(1024)S(1)} %get-tuple-element.191, f32[]{:T(128)} %get-tuple-element.105), channel_id=1, replica_groups=mesh['dp'=16,'rows'=2] {'dp','rows'}, use_global_device_ids=true, to_apply=%region_1.0 | all-reduce | flops 1493 | bytes 11944 | tf_op jit(solution)/shard_map/psum | solution.py:99
  122.0 40.6 %psum.141 = f32[1492]{0:T(1024)S(1)} all-reduce(f32[1492]{0:T(1024)S(1)} %fusion), channel_id=1, replica_groups=mesh['dp'=16,'rows'=2] {'dp','rows'}, use_global_device_ids=true, to_apply=%region_5.0 | all-reduce | flops 1492 | bytes 11936 | tf_op jit(solution)/shard_map/psum | solution.py:104
  279.0 76.8 %slice_reduce_fusion.2 = (bf16[373,1492]{0,1:T(8,128)(2,1)}, bf16[373,1492]{0,1:T(8,128)(2,1)}, bf16[373,1492]{0,1:T(8,128)(2,1)}, bf16[373,1492]{0,1:T(8,128)(2...) fusion(bf16[3,3,373,1492]{2,1,0,3:T(4,128)(2,1)} %all-gather.12, ...), kind=kLoop, calls=%fused_computation.61 | loop fusion | bytes 20034576 | tf_op jit(solution)/shard_map/slice | solution.py:57
  443.5 40.0 %psum.142 = f32[1492]{0:T(1024)S(1)} all-reduce(f32[1492]{0:T(1024)S(1)} %multiply_reduce_fusion.4), channel_id=1, replica_groups=mesh['dp'=16,'rows'=2] {'dp','rows'}, use_global_device_ids=true, to_apply=%region_7.8 | all-reduce | flops 1492 | bytes 11936 | tf_op jit(solution)/shard_map/psum | solution.py:99
  487.1 40.9 %psum.143 = f32[1492]{0:T(1024)S(1)} all-reduce(f32[1492]{0:T(1024)S(1)} %fusion.1), channel_id=1, replica_groups=mesh['dp'=16,'rows'=2] {'dp','rows'}, use_global_device_ids=true, to_apply=%region_9.10 | all-reduce | flops 1492 | bytes 11936 | tf_op jit(solution)/shard_map/psum | solution.py:104
  555.4 11.1 multiply_reduce_fusion.3
  566.5 39.2 %psum.146 = f32[1492]{0:T(1024)S(1)} all-reduce(f32[1492]{0:T(1024)S(1)} %get-tuple-element.193), channel_id=1, replica_groups=mesh['dp'=16,'rows'=2] {'dp','rows'}, use_global_device_ids=true, to_apply=%region_15.16 | all-reduce | flops 1492 | bytes 11936 | tf_op jit(solution)/shard_map/psum | solution.py:99
  609.5 40.9 %psum.147 = f32[1492]{0:T(1024)S(1)} all-reduce(f32[1492]{0:T(1024)S(1)} %fusion.2), channel_id=1, replica_groups=mesh['dp'=16,'rows'=2] {'dp','rows'}, use_global_device_ids=true, to_apply=%region_17.18 | all-reduce | flops 1492 | bytes 11936 | tf_op jit(solution)/shard_map/psum | solution.py:104
  651.1 10.7 fusion.178
  661.8 39.5 %all-reduce.17 = (f32[1492]{0:T(1024)S(1)}, f32[1492]{0:T(1024)S(1)}) all-reduce(f32[1492]{0:T(1024)S(1)} %get-tuple-element.104, f32[1492]{0:T(1024)S(1)} %get-tuple-element.103), channel_id=1, replica_groups=mesh['dp'=16,'rows'=2] {'dp','rows'}, use_global_device_ids=true, to_apply=%region_21.22 | all-reduce | flops 2984 | bytes 23872 | tf_op jit(solution)/shard_map/psum | solution.py:111
  707.6 10.7 fusion.191
  740.0 10.1 fusion.177
  750.1 41.5 %all-reduce.16 = (f32[1492]{0:T(1024)S(1)}, f32[1492]{0:T(1024)S(1)}) all-reduce(f32[1492]{0:T(1024)S(1)} %get-tuple-element.102, f32[1492]{0:T(1024)S(1)} %get-tuple-element.101), channel_id=1, replica_groups=mesh['dp'=16,'rows'=2] {'dp','rows'}, use_global_device_ids=true, to_apply=%region_29.30 | all-reduce | flops 2984 | bytes 23872 | tf_op jit(solution)/shard_map/psum | solution.py:336
  816.0 12.0 fusion.172
  977.8 13.8 maximum_add_fusion
  991.6 23.0 copy.532
  1014.6 23.6 add.365
  1038.2 9.9 copy.533
  1060.5 14.1 dynamic-update-slice.12
  1074.6 14.0 dynamic-update-slice.13
  1088.6 190.8 %while.1 = (u32[]{:T(128)}, f32[2,3357,746]{2,1,0:T(8,128)}, f32[5008644]{0:T(1024)}, u32[]{}, u32[]{}, /*index=5*/u32[]{}, u32[]{}, u32[]{}) while((u32[]{:T(128)}, f32[2,3357,746]{2,1,0:T(8,128)}, f32[5008644]{0:T(1024)}, u32[]{}, u32[]{}, /*index=5*/u32[]{}, u32[]{}, u32[]{}) %tuple.96), condition=%wide.cond, body=%wide.body.sunk | while | flops 9 | bytes 25155308
  1099.8 36.4 %dynamic-update-slice.16 = f32[5008644]{0:T(1024)} dynamic-update-slice(f32[5008644]{0:T(1024)} %get-tuple-element.236, f32[1048130]{0:T(1024)} %reshape.663, u32[]{:T(128)S(6)} %add.566) | dynamic-update-slice | bytes 8385044
  1147.3 36.5 %dynamic-update-slice.16 = f32[5008644]{0:T(1024)} dynamic-update-slice(f32[5008644]{0:T(1024)} %get-tuple-element.236, f32[1048130]{0:T(1024)} %reshape.663, u32[]{:T(128)S(6)} %add.566) | dynamic-update-slice | bytes 8385044
  1195.0 36.6 %dynamic-update-slice.16 = f32[5008644]{0:T(1024)} dynamic-update-slice(f32[5008644]{0:T(1024)} %get-tuple-element.236, f32[1048130]{0:T(1024)} %reshape.663, u32[]{:T(128)S(6)} %add.566) | dynamic-update-slice | bytes 8385044
  1242.8 36.6 %dynamic-update-slice.16 = f32[5008644]{0:T(1024)} dynamic-update-slice(f32[5008644]{0:T(1024)} %get-tuple-element.236, f32[1048130]{0:T(1024)} %reshape.663, u32[]{:T(128)S(6)} %add.566) | dynamic-update-slice | bytes 8385044
  1298.6 15.8 reshape.652
  1314.5 12.8 reshape.505
  1346.7 30.2 reshape.510
  1376.9 77.3 %dynamic-update-slice.7 = f32[2,5286902]{1,0:T(2,128)} dynamic-update-slice(f32[2,5286902]{1,0:T(2,128)} %custom-call, f32[2,1113032]{1,0:T(2,128)} %reshape.505, s32[]{} %constant.112, s32[]{} %constant.112) | dynamic-update-slice | bytes 17808516
  1454.2 20.9 dynamic-update-slice.8
  1475.2 22.1 dynamic-update-slice.9
  1497.3 189.2 %dynamic-update-slice.10 = f32[2,5286902]{1,0:T(2,128)} dynamic-update-slice(f32[2,5286902]{1,0:T(2,128)} %dynamic-update-slice.9, f32[2,2504322]{1,0:T(2,128)} %reshape.510, s32[]{} %constant.112, s32[]{} %constant.115) | dynamic-update-slice | bytes 40069156
  1857.9 39.2 %all-reduce.15 = (f32[1492]{0:T(1024)S(1)}, f32[1492]{0:T(1024)S(1)}) all-reduce(f32[1492]{0:T(1024)S(1)} %get-tuple-element.100, f32[1492]{0:T(1024)S(1)} %get-tuple-element.99), channel_id=1, replica_groups=mesh['dp'=16,'rows'=2] {'dp','rows'}, use_global_device_ids=true, to_apply=%region_33.34 | all-reduce | flops 2984 | bytes 23872 | tf_op jit(solution)/shard_map/psum | solution.py:111
  1919.0 9.9 copy.534
  1928.9 15.8 reshape.658
  1944.7 12.9 reshape.512
  1957.6 84.4 %dynamic-update-slice.11 = f32[2,5286902]{1,0:T(2,128)} dynamic-update-slice(f32[2,5286902]{1,0:T(2,128)} %dynamic-update-slice.10, f32[2,1113032]{1,0:T(2,128)} %reshape.512, s32[]{} %constant.112, s32[]{} %constant.116) | dynamic-update-slice | bytes 17808516 | tf_op jit(solution)/shard_map/concatenate | solution.py:140
  2042.1 31.4 pad.23
  2073.5 93.2 %reshape.660 = f32[10573824]{0:T(1024)} reshape(f32[2,5286912]{1,0:T(2,128)} %pad.23) | data formatting | bytes 84590592
  2166.7 43.3 %reshape.513 = f32[2,16,330432]{2,1,0:T(8,128)} reshape(f32[10573824]{0:T(1024)} %reshape.660) | data formatting | bytes 84590592 | tf_op jit(solution)/shard_map/reshape | solution.py:135
  2210.0 58.1 %copy.819 = f32[2,16,330432]{2,0,1:T(2,128)} copy(f32[2,16,330432]{2,1,0:T(8,128)} %reshape.513) | data formatting | bytes 84590592 | tf_op jit(solution)/shard_map/reshape | solution.py:135
  2268.1 68.1 %reshape.514 = f32[32,330432]{1,0:T(8,128)} reshape(f32[16,2,330432]{2,1,0:T(2,128)} %bitcast.375) | data formatting | bytes 84590592 | tf_op jit(solution)/shard_map/reshape | solution.py:135
  2336.2 671.1 %all-reduce.23 = (bf16[32,330432]{1,0:T(8,128)(2,1)}, f32[373]{0:T(512)}, f32[1492]{0:T(1024)S(1)}) all-reduce(f32[32,330432]{1,0:T(8,128)} %reshape.514, f32[373]{0:T(512)S(1)} %copy-done.119, f32[1492]{0:T(1024)S(1)} %copy-done.97), channel_id=2, replica_groups=mesh['dp'=16,'rows'=2] {'dp','rows'}, use_global_device_ids=true, to_apply=%region_34.35.clone | all-reduce | flops 10575689 | bytes 63457864
  3058.9 185.4 %all-gather.22.cloned.1.call-done = bf16[16,1,330432]{2,1,0:T(2,128)(2,1)} async-done(((bf16[1,1,330432]{2,1,0:T(2,128)(2,1)}), bf16[16,1,330432]{2,1,0:T(2,128)(2,1)}) %all-gather.22.cloned.1.call-update) | async-done | bytes 10573840 | tf_op jit(solution)/shard_map/all_gather | solution.py:143
  3244.2 226.2 %convert_reduce_fusion = f32[16,330432]{1,0:T(8,128)} fusion(bf16[16,1,330432]{2,1,0:T(2,128)(2,1)} %all-gather.22.cloned.1.call-done), kind=kLoop, calls=%fused_computation.1 | loop fusion | flops 5286912 | bytes 31721472 | tf_op jit(solution)/shard_map/reshape | solution.py:145
  3470.4 22.1 reshape.525
  3518.9 18.4 reshape.518
  (603 shorter events, 878.4 us)
Async XLA Ops:
  7.2 41.3 %all-gather.18.cloned.1.call-start = ((), (), s32[]{:S(2)}) async-start(), calls=%async_computation.3 | async-start | bytes 1732608 | tf_op jit(solution)/shard_map/all_gather | solution.py:185
  9.4 41.9 %all-gather.16.cloned.1.call-start = ((), (), s32[]{:S(2)}) async-start(), calls=%async_computation.2 | async-start | bytes 1732608 | tf_op jit(solution)/shard_map/all_gather | solution.py:184
  10.1 43.9 %all-gather.14.cloned.1.call-start = ((), (), s32[]{:S(2)}) async-start(), calls=%async_computation.1 | async-start | bytes 6893568 | tf_op jit(solution)/shard_map/all_gather | solution.py:181
  10.9 183.0 %all-gather.20.cloned.1.call-start = ((), (), s32[]{:S(2)}) async-start(), calls=%async_computation.4 | async-start | bytes 6893568 | tf_op jit(solution)/shard_map/all_gather | solution.py:183
  11.4 267.6 %all-gather.12.cloned.1.call-start = ((), (), s32[]{:S(2)}) async-start(), calls=%async_computation | async-start | bytes 20625408 | tf_op jit(solution)/shard_map/all_gather | solution.py:182
  24.7 8.0 copy-start.85
  24.7 3219.5 %all-gather.22.cloned.1.call-start = ((), (), s32[]{:S(2)}) async-start(), calls=%async_computation.5 | async-start | bytes 22473728 | tf_op jit(solution)/shard_map/all_gather | solution.py:143
  37.9 30.1 copy-start.57
  37.9 125.8 %copy-start.92 = (f32[1492]{0:T(1024)}, f32[1492]{0:T(1024)S(1)}, u32[]{:S(2)}) copy-start(f32[1492]{0:T(1024)S(1)} %convert_element_type.106) | copy-start | bytes 17908
  38.0 125.8 %copy-start.94 = (f32[1492]{0:T(1024)}, f32[1492]{0:T(1024)S(1)}, u32[]{:S(2)}) copy-start(f32[1492]{0:T(1024)S(1)} %convert_element_type.105) | copy-start | bytes 17908
  47.5 6.5 copy-start.115
  48.5 744.5 %copy-start.86 = (f32[752]{0:T(1024)}, f32[752]{0:T(1024)S(1)}, u32[]{:S(2)}) copy-start(f32[752]{0:T(1024)S(1)} %get-tuple-element.106) | copy-start | bytes 9028
  60.7 7.3 copy-start.80
  118.8 45.0 %copy-start.88 = (f32[1492]{0:T(1024)}, f32[1492]{0:T(1024)S(1)}, u32[]{:S(2)}) copy-start(f32[1492]{0:T(1024)S(1)} %broadcast_divide_fusion.8) | copy-start | bytes 17908
  178.2 28.8 collective-permute-start.1
  179.5 27.5 collective-permute-start
  190.9 53.1 %collective-permute-start.2 = (bf16[5,1,12,1492]{3,2,1,0:T(8,128)(2,1)}, bf16[5,1,12,1492]{3,2,1,0:T(8,128)(2,1)S(1)}, u32[]{:S(2)}, u32[]{:S(2)}) collective-permute-start(bf16[5,1,12,1492]{3,2,1,0:T(8,128)(2,1)} %get-tuple-element.181), channel_id=1, source_target_pairs={{0,1},{2,3},{4,5},{6,7},{8,9},{10,11},{12,13},{14,15},{16,17},{18,... | collective-permute-start | bytes 537128 | tf_op jit(solution)/shard_map/ppermute | solution.py:15
  192.2 51.8 %collective-permute-start.3 = (bf16[5,1,12,1492]{3,2,1,0:T(8,128)(2,1)}, bf16[5,1,12,1492]{3,2,1,0:T(8,128)(2,1)S(1)}, u32[]{:S(2)}, u32[]{:S(2)}) collective-permute-start(bf16[5,1,12,1492]{3,2,1,0:T(8,128)(2,1)} %get-tuple-element.182), channel_id=1, source_target_pairs={{1,0},{3,2},{5,4},{7,6},{9,8},{11,10},{13,12},{15,14},{17,16},{19,... | collective-permute-start | bytes 537128 | tf_op jit(solution)/shard_map/ppermute | solution.py:18
  372.0 50.7 %copy-start.6 = (bf16[373,4,373]{0,2,1:T(8,128)(2,1)}, bf16[373,4,373]{0,2,1:T(8,128)(2,1)S(1)}, u32[]{:S(2)}) copy-start(bf16[373,4,373]{0,2,1:T(8,128)(2,1)S(1)} %reshape_squeeze.18) | copy-start | bytes 3339100
  372.6 52.7 %copy-start.4 = (bf16[373,4,373]{0,2,1:T(8,128)(2,1)}, bf16[373,4,373]{0,2,1:T(8,128)(2,1)S(1)}, u32[]{:S(2)}) copy-start(bf16[373,4,373]{0,2,1:T(8,128)(2,1)S(1)} %reshape_squeeze.19) | copy-start | bytes 3339100
  374.8 36.4 %copy-start.2 = (bf16[373,4,373]{0,2,1:T(8,128)(2,1)}, bf16[373,4,373]{0,2,1:T(8,128)(2,1)S(1)}, u32[]{:S(2)}) copy-start(bf16[373,4,373]{0,2,1:T(8,128)(2,1)S(1)} %reshape_squeeze.26) | copy-start | bytes 3339100
  484.2 44.5 %copy-start.96 = (f32[1492]{0:T(1024)S(1)}, f32[1492]{0:T(1024)}, u32[]{:S(2)}) copy-start(f32[1492]{0:T(1024)} %convert_element_type.108) | copy-start | bytes 17908
  536.2 8.5 copy-start.117
  536.2 8.5 copy-start.120
  555.4 11.1 copy-start.31
  701.3 6.3 copy-start.99
  707.6 10.7 copy-start.84
  791.6 7.3 copy-start.103
  791.6 7.3 copy-start.105
  803.5 83.4 %copy-start.25 = (bf16[5,6,12,1492]{3,2,1,0:T(8,128)(2,1)}, bf16[5,6,12,1492]{3,2,1,0:T(8,128)(2,1)S(1)}, u32[]{:S(2)}) copy-start(bf16[5,6,12,1492]{3,2,1,0:T(8,128)(2,1)S(1)} %reshape.491) | copy-start | bytes 3222724
  811.6 81.9 %copy-start.27 = (bf16[1,14,28,1492]{3,2,1,0:T(8,128)(2,1)}, bf16[1,14,28,1492]{3,2,1,0:T(8,128)(2,1)S(1)}, u32[]{:S(2)}) copy-start(bf16[1,14,28,1492]{3,2,1,0:T(8,128)(2,1)S(1)} %reshape.480) | copy-start | bytes 3509188
  828.0 8.1 copy-start.22
  828.0 8.1 copy-start.54
  887.7 876.3 %collective-permute-start.7 = (bf16[5,1,12,1492]{3,2,1,0:T(8,128)(2,1)}, bf16[5,1,12,1492]{3,2,1,0:T(8,128)(2,1)}, u32[]{:S(2)}, u32[]{:S(2)}) collective-permute-start(bf16[5,1,12,1492]{3,2,1,0:T(8,128)(2,1)} %get-tuple-element.177), channel_id=1, source_target_pairs={{1,0},{3,2},{5,4},{7,6},{9,8},{11,10},{13,12},{15,14},{17,16},{19,... | collective-permute-start | bytes 537128 | tf_op jit(solution)/shard_map/ppermute | solution.py:18
  889.0 875.0 %collective-permute-start.6 = (bf16[5,1,12,1492]{3,2,1,0:T(8,128)(2,1)}, bf16[5,1,12,1492]{3,2,1,0:T(8,128)(2,1)}, u32[]{:S(2)}, u32[]{:S(2)}) collective-permute-start(bf16[5,1,12,1492]{3,2,1,0:T(8,128)(2,1)} %get-tuple-element.178), channel_id=1, source_target_pairs={{0,1},{2,3},{4,5},{6,7},{8,9},{10,11},{12,13},{14,15},{16,17},{18,... | collective-permute-start | bytes 537128 | tf_op jit(solution)/shard_map/ppermute | solution.py:15
  894.2 792.3 %collective-permute-start.5 = (bf16[1,1,28,1492]{3,2,1,0:T(8,128)(2,1)}, bf16[1,1,28,1492]{3,2,1,0:T(8,128)(2,1)}, u32[]{:S(2)}, u32[]{:S(2)}) collective-permute-start(bf16[1,1,28,1492]{3,2,1,0:T(8,128)(2,1)} %get-tuple-element.186), channel_id=1, source_target_pairs={{1,0},{3,2},{5,4},{7,6},{9,8},{11,10},{13,12},{15,14},{17,16},{19,... | collective-permute-start | bytes 250664 | tf_op jit(solution)/shard_map/ppermute | solution.py:18
  895.5 791.0 %collective-permute-start.4 = (bf16[1,1,28,1492]{3,2,1,0:T(8,128)(2,1)}, bf16[1,1,28,1492]{3,2,1,0:T(8,128)(2,1)}, u32[]{:S(2)}, u32[]{:S(2)}) collective-permute-start(bf16[1,1,28,1492]{3,2,1,0:T(8,128)(2,1)} %get-tuple-element.185), channel_id=1, source_target_pairs={{0,1},{2,3},{4,5},{6,7},{8,9},{10,11},{12,13},{14,15},{16,17},{18,... | collective-permute-start | bytes 250664 | tf_op jit(solution)/shard_map/ppermute | solution.py:15
  1048.1 6.9 copy-start
  1060.5 14.1 copy-start.56
  1088.6 191.4 %copy-start.118 = (f32[373]{0:T(512)S(1)}, f32[373]{0:T(512)}, u32[]{:S(2)}) copy-start(f32[373]{0:T(512)} %get-tuple-element.197) | copy-start | bytes 4480
  1376.9 77.3 %copy-start.53 = (f32[2,278258]{1,0:T(2,128)S(1)}, f32[2,278258]{1,0:T(2,128)}, u32[]{:S(2)}) copy-start(f32[2,278258]{1,0:T(2,128)} %reshape.507) | copy-start | bytes 6678196
  1497.3 189.2 %copy-start.28 = (bf16[1,14,28,1492]{3,2,1,0:T(8,128)(2,1)S(1)}, bf16[1,14,28,1492]{3,2,1,0:T(8,128)(2,1)}, u32[]{:S(2)}) copy-start(bf16[1,14,28,1492]{3,2,1,0:T(8,128)(2,1)} %copy-done.27) | copy-start | bytes 3509188
  1850.0 47.8 %copy-start.87 = (f32[752]{0:T(1024)S(1)}, f32[752]{0:T(1024)}, u32[]{:S(2)}) copy-start(f32[752]{0:T(1024)} %copy-done.86) | copy-start | bytes 9028
  1850.0 47.8 %copy-start.98 = (f32[1492]{0:T(1024)S(1)}, f32[1492]{0:T(1024)}, u32[]{:S(2)}) copy-start(f32[1492]{0:T(1024)} %get-tuple-element.135) | copy-start | bytes 17908
  1897.8 6.5 copy-start.58
  1897.8 6.5 copy-start.81
  2268.1 68.1 %copy-start.97 = (f32[1492]{0:T(1024)S(1)}, f32[1492]{0:T(1024)}, u32[]{:S(2)}) copy-start(f32[1492]{0:T(1024)} %broadcast_multiply_fusion) | copy-start | bytes 17908
  2268.1 68.1 %copy-start.119 = (f32[373]{0:T(512)S(1)}, f32[373]{0:T(512)}, u32[]{:S(2)}) copy-start(f32[373]{0:T(512)} %broadcast_multiply_fusion.1) | copy-start | bytes 4480
  (98 other events, 276.7 us)
Sparse Core Ops, SparseCore 0:
  10.1 11.8 all-gather.17
  23.6 10.3 all-gather.15
  35.5 15.4 all-gather.13
  52.4 15.4 all-gather.19
  69.9 27.1 all-gather.11
  3012.4 231.7 all-gather.21
where the time goes:
time: 3610 us; the launch traced here: 3560 us
  local copies, waits for them, and re-layouts  1700 us (47%)
  blocking collectives  1050 us (29%)
  other arithmetic  355 us (10%)
  matrix products  235 us (7%)
  waiting for transfers between devices  187 us (5%)
    unnamed x307, local copies, waits for them, and re-layouts  723 us
    unnamed x3, blocking collectives  678 us
    reshape x1, other arithmetic, reduce_all(): gathered = lax.all_gather(owned.astype(jnp.bfloat16), 'dp', axis=0, tiled...  226 us
    all_gather x1, waiting for transfers between devices, reduce_all(): lax.all_gather(owned.astype(jnp.bfloat16), 'dp', axis=0, tiled=True)  185 us
    reshape x3, local copies, waits for them, and re-layouts, spread_blocks(): padded.reshape(2, blocks, width).transpose(1, 0, 2)  170 us
    psum x3, blocking collectives, norm_forward(): lax.psum(jnp.sum(pixel_mask * centered * centered, 0), ('dp', 'rows'))  122 us
    psum x3, blocking collectives, norm_forward(): lax.psum((jnp.sum(values * pixel_mask, 0), local_count), ('dp', 'rows'))  121 us
    reshape x9, local copies, waits for them, and re-layouts, halve_term(): local_term.reshape(-1, 2, last_dim // 2).transpose(1, 0, 2).reshape(2, -1)  87.9 us
  transfers between devices with their start and end apart: 14, of which 1 were waited for; matrix products, arithmetic and copies ran while one was open for 30% of the time, Pallas kernels for 0%

commit v1 on v0

v1 whole, which is shorter than its diff:
```python
import functools

import jax
import jax.numpy as jnp
from jax import lax
from jax.experimental import pallas as pl
from jax.experimental.pallas import tpu as pltpu
from jax.sharding import PartitionSpec as P

EPSILON = 1e-05
MESH = pl.DeviceIdType.MESH
F32 = jnp.float32
BF16 = jnp.bfloat16
ANY = pl.BlockSpec(memory_space=pl.ANY)
VMEM = pl.BlockSpec(memory_space=pltpu.VMEM)
LANE = 128
TILE = 64
VMEM_BYTES = 62 * 1024 * 1024


def round_up(value, step):
    return -(-value // step) * step


class Plan:
    def __init__(self, glob_shape, small_shape, group_width, dp):
        self.glob_height, self.glob_side = glob_shape[1], glob_shape[2]
        self.slots, self.small_height, self.small_side = small_shape[:3]
        self.channels = glob_shape[3]
        self.glob_width = round_up(self.glob_side + 1, 32)
        self.small_width = round_up(self.small_side + 1, 16)
        self.glob_own = self.glob_height * self.glob_width
        self.slot_own = self.small_height * self.small_width
        self.own = self.glob_own + self.slots * self.slot_own
        self.glob_all = 2 * self.glob_own
        self.slot_all = 2 * self.slot_own
        self.all = 2 * self.own
        self.glob_base = self.glob_width
        self.small_base = self.glob_all + 2 * self.glob_width
        self.slot_conv = self.slot_all + self.small_width
        self.small_conv = self.slots * self.slot_conv
        self.conv = self.small_base + self.small_conv
        self.width = group_width
        self.group = round_up(group_width, LANE)
        self.half = 2 * self.group
        self.half_real = self.channels // 2
        self.dp = dp
        self.glob_tiles = self.glob_all // TILE
        self.slot_tiles = self.slot_all // TILE
        self.slot_rows = round_up(1 + self.slots, 8)
        self.glob_area = float(2 * self.glob_height * self.glob_side)
        self.slot_area = float(2 * self.small_height * self.small_side)

    def own_pieces(self, core):
        pieces = [(pl.multiple_of(core * self.glob_own, 16), 0, self.glob_own)]
        for slot in range(self.slots):
            place = self.glob_all + slot * self.slot_all + core * self.slot_own
            pieces.append(
                (pl.multiple_of(place, 16), self.glob_own + slot * self.slot_own, self.slot_own)
            )
        return pieces

    def sweep(self, body, carry):
        def glob_step(tile, state):
            start = pl.multiple_of(tile * TILE, TILE)
            return body(start, pl.multiple_of(self.glob_base + start, 16), 0, state)

        def slot_step(tile, state):
            slot = tile // self.slot_tiles
            start = pl.multiple_of(self.glob_all + tile * TILE, TILE)
            place = self.small_base + tile * TILE + slot * self.small_width
            return body(start, pl.multiple_of(place, 16), 1 + slot, state)

        carry = lax.fori_loop(0, self.glob_tiles, glob_step, carry)
        return lax.fori_loop(0, self.slots * self.slot_tiles, slot_step, carry)

    def segments(self):
        return (
            (self.glob_base, self.glob_all, self.glob_width),
            (self.small_base, self.small_conv - self.small_width, self.small_width),
        )


def sigmoid(value):
    return 0.5 * jnp.tanh(0.5 * value) + 0.5


def rows_down(tile):
    return jnp.sum(tile.reshape(tile.shape[0] // 8, 8, tile.shape[1]), 0)


def widen(mask, lanes):
    return jnp.concatenate([mask] * (lanes // mask.shape[1]), 1)


def dot(left, right):
    return jnp.dot(left, right, preferred_element_type=F32)


def dot_nt(left, right):
    return lax.dot_general(left, right, (((1,), (1,)), ((), ())), preferred_element_type=F32)


def dot_tn(left, right):
    return lax.dot_general(left, right, (((0,), (0,)), ((), ())), preferred_element_type=F32)


def split_dot(left, right, nt=False):
    high = left.astype(BF16)
    low = (left - high.astype(F32)).astype(BF16)
    call = dot_nt if nt else dot
    return call(high, right) + call(low, right)


def entry_barrier(n, me, core):
    barrier = pltpu.get_barrier_semaphore()

    def greet(step, carry):
        pl.semaphore_signal(
            barrier, inc=1, device_id=(lax.rem(me + step, n), core), device_id_type=MESH
        )
        return carry

    lax.fori_loop(1, n, greet, 0)
    pl.semaphore_signal(barrier, inc=1, device_id=(me, 1 - core), device_id_type=MESH)
    pl.semaphore_wait(barrier, n)


class Spread:
    def __init__(self, n, me, core, source, slots, send, recv):
        self.n, self.me, self.core = n, me, core
        self.source, self.slots, self.send, self.recv = source, slots, send, recv

    def copy(self, step):
        return pltpu.make_async_remote_copy(
            src_ref=self.source,
            dst_ref=self.slots.at[self.me],
            send_sem=self.send.at[step],
            recv_sem=self.recv.at[step],
            device_id=(lax.rem(self.me + step, self.n), self.core),
            device_id_type=MESH,
        )

    def start(self):
        def begin(step, carry):
            self.copy(step).start()
            return carry

        lax.fori_loop(1, self.n, begin, 0)
        self.slots[pl.ds(self.me, 1)] = self.source[...][None]

    def wait(self):
        def end(step, carry):
            self.copy(step).wait()
            return carry

        lax.fori_loop(1, self.n, end, 0)


def to_partner(me, core, source, target, send, recv):
    return pltpu.make_async_remote_copy(
        src_ref=source,
        dst_ref=target,
        send_sem=send,
        recv_sem=recv,
        device_id=(me, 1 - core),
        device_id_type=MESH,
    )


def merge_moments(slots, n, lanes):
    def add(step, carry):
        total, count = carry
        return (total + slots[step, :, :lanes], count + slots[step, :, 2 * lanes : 2 * lanes + LANE])

    total, count = lax.fori_loop(
        0, n, add, (jnp.zeros((1, lanes), F32), jnp.zeros((1, LANE), F32))
    )
    wide_count = widen(count, lanes)
    mean = total / wide_count

    def spread(step, carry):
        own_count = widen(slots[step, :, 2 * lanes : 2 * lanes + LANE], lanes)
        gap = slots[step, :, :lanes] / own_count - mean
        return carry + slots[step, :, lanes : 2 * lanes] + own_count * gap * gap

    squares = lax.fori_loop(0, n, spread, jnp.zeros((1, lanes), F32))
    return mean, squares / wide_count, wide_count


def local_moments(plan, values, mask, which, count):
    lanes = plan.half

    def add(start, place, crop, carry):
        row = start if which == "all" else place
        tile = values[pl.ds(row, TILE), :] * widen(mask[pl.ds(start, TILE), :], lanes)
        return carry + rows_down(tile)

    total = jnp.sum(plan.sweep(add, jnp.zeros((8, lanes), F32)), 0, keepdims=True)
    mean = total / count

    def spread(start, place, crop, carry):
        row = start if which == "all" else place
        gap = (values[pl.ds(row, TILE), :] - mean) * widen(mask[pl.ds(start, TILE), :], lanes)
        return carry + rows_down(gap * gap)

    squares = jnp.sum(plan.sweep(spread, jnp.zeros((8, lanes), F32)), 0, keepdims=True)
    return total, squares


GAIN_ONE, SHIFT_ONE, GAIN_TWO, SHIFT_TWO, EXCITE_BIAS, SQUEEZE_BIAS, COUNT = range(7)
MEAN_ONE, INVERSE_ONE, MEAN_TWO, INVERSE_TWO, TOTAL = range(5)


def forward_kernel(
    plan,
    x_own,
    w_in,
    w_mid_hbm,
    k_out,
    w_in_hbm,
    vec,
    vec_three,
    mask,
    w_squeeze,
    w_excite,
    x_out,
    pre_one_out,
    act_one_out,
    pre_two_out,
    act_three_out,
    k_out_all,
    w_in_all,
    vec_three_all,
    stats,
    pooled_out,
    excite_out,
    squeeze_pre_out,
    x_all,
    pre_one,
    shifted,
    w_mid,
    pre_two,
    act_two,
    act_three,
    pay_one,
    slots_one,
    pay_two,
    slots_two,
    squeeze_send,
    squeeze_recv,
    local_sem,
    send_sem,
    recv_sem,
    spread_send,
    spread_recv,
):
    n, half, group = plan.dp, plan.half, plan.group
    me, core = lax.axis_index("dp"), lax.axis_index("rows")
    pieces = plan.own_pieces(core)
    entry_barrier(n, me, core)

    def local(source, target, index):
        copy = pltpu.make_async_copy(source, target, local_sem.at[index])
        copy.start()
        return copy

    def partner(source, target, index):
        copy = to_partner(me, core, source, target, send_sem.at[index], recv_sem.at[index])
        copy.start()
        return copy

    x_local, x_remote = [], []
    for index, (place, start, length) in enumerate(pieces):
        source = x_own.at[:, pl.ds(start, length), :]
        target = x_all.at[:, pl.ds(place, length), :]
        x_remote.append(partner(source, target, index))
        x_local.append(local(source, target, index))
    base = len(pieces)
    mid_copy = local(w_mid_hbm, w_mid, base)
    others = [
        local(k_out, k_out_all.at[core], base + 1),
        local(w_in_hbm, w_in_all.at[core], base + 2),
        local(vec_three, vec_three_all.at[core], base + 3),
    ]
    others += [
        partner(k_out, k_out_all.at[core], base),
        partner(w_in_hbm, w_in_all.at[core], base + 1),
        partner(vec_three, vec_three_all.at[core], base + 2),
    ]
    for side in range(2):
        shifted[side, : plan.glob_base, :] = jnp.zeros((plan.glob_base, 3 * group), BF16)
        shifted[side, plan.glob_base + plan.glob_all : plan.small_base, :] = jnp.zeros(
            (plan.glob_width, 3 * group), BF16
        )
        for slot in range(plan.slots):
            low = plan.small_base + slot * plan.slot_conv + plan.slot_all
            shifted[side, low : low + plan.small_width, :] = jnp.zeros(
                (plan.small_width, 3 * group), BF16
            )

    def product(owner):
        place = pl.multiple_of(owner * plan.glob_own, 16)
        rows = pl.ds(place, plan.glob_own)
        pre_one[rows, :] = dot(x_all[0, rows, :], w_in[0]) + dot(x_all[1, rows, :], w_in[1])
        places = [spot for spot, _, _ in plan.own_pieces(owner)[1:]]
        sides = [
            jnp.concatenate([x_all[side, pl.ds(spot, plan.slot_own), :] for spot in places], 0)
            for side in range(2)
        ]
        result = dot(sides[0], w_in[0]) + dot(sides[1], w_in[1])
        for slot, spot in enumerate(places):
            pre_one[pl.ds(spot, plan.slot_own), :] = result[
                slot * plan.slot_own : (slot + 1) * plan.slot_own
            ]

    for copy in x_local:
        copy.wait()
    product(core)
    for copy in x_remote:
        copy.wait()
    product(1 - core)
    saves = [
        local(x_all, x_out, base + 4),
        local(pre_one, pre_one_out, base + 5),
    ]

    chip_count = vec[COUNT : COUNT + 1, :]

    def statistics(values, which, pay, slots, index):
        total, squares = local_moments(plan, values, mask, which, chip_count)
        pay[:, :half] = total
        pay[:, half : 2 * half] = squares
        pay[:, 2 * half :] = chip_count[:, :LANE]
        spread = Spread(n, me, core, pay, slots, spread_send.at[index], spread_recv.at[index])
        spread.start()
        spread.wait()
        mean, variance, count = merge_moments(slots, n, half)
        return mean, lax.rsqrt(variance + EPSILON), count

    mean, inverse, count = statistics(pre_one, "all", pay_one, slots_one, 0)
    stats[...] = jnp.zeros_like(stats)
    stats[MEAN_ONE : MEAN_ONE + 1, :] = mean
    stats[INVERSE_ONE : INVERSE_ONE + 1, :] = inverse
    stats[TOTAL : TOTAL + 1, :] = count
    scale = inverse * vec[GAIN_ONE : GAIN_ONE + 1, :]
    shift = vec[SHIFT_ONE : SHIFT_ONE + 1, :]

    def activate_one(start, place, crop, carry):
        norm = (pre_one[pl.ds(start, TILE), :] - mean) * scale + shift
        act = norm * sigmoid(norm) * widen(mask[pl.ds(start, TILE), :], half)
        before = pltpu.roll(act, 1, 0)
        after = pltpu.roll(act, TILE - 1, 0)
        for tap, value in enumerate((before, act, after)):
            for side in range(2):
                shifted[side, pl.ds(place, TILE), tap * group : (tap + 1) * group] = value[
                    :, side * group : (side + 1) * group
                ].astype(BF16)
        return carry

    plan.sweep(activate_one, 0)
    for side in range(2):
        saves.append(
            local(
                shifted.at[side, :, group : 2 * group],
                act_one_out.at[:, side * group : (side + 1) * group],
                base + 6 + side,
            )
        )
    mid_copy.wait()

    for low, length, width in plan.segments():
        for side in range(2):
            lanes = slice(side * group, (side + 1) * group)
            block = length // 2
            for part in range(2):
                at = low + part * block
                total = None
                for tap in range(3):
                    first = at + (tap - 1) * width
                    term = dot(shifted[side, first : first + block, :], w_mid[tap, :, lanes])
                    total = term if total is None else total + term
                pre_two[at : at + block, lanes] = total
    saves.append(local(pre_two, pre_two_out, base + 8))

    mean_two, inverse_two, _ = statistics(pre_two, "conv", pay_two, slots_two, 1)
    stats[MEAN_TWO : MEAN_TWO + 1, :] = mean_two
    stats[INVERSE_TWO : INVERSE_TWO + 1, :] = inverse_two
    scale_two = inverse_two * vec[GAIN_TWO : GAIN_TWO + 1, :]
    shift_two = vec[SHIFT_TWO : SHIFT_TWO + 1, :]
    pooled_out[...] = jnp.zeros_like(pooled_out)

    def activate_two(start, place, crop, carry):
        norm = (pre_two[pl.ds(place, TILE), :] - mean_two) * scale_two + shift_two
        act = norm * sigmoid(norm) * widen(mask[pl.ds(start, TILE), :], half)
        act_two[pl.ds(start, TILE), :] = act
        pooled_out[pl.ds(crop, 1), :] += jnp.sum(act, 0, keepdims=True)
        return carry

    plan.sweep(activate_two, 0)
    pooled_out[:1, :] = pooled_out[:1, :] * (1.0 / plan.glob_area)
    pooled_out[1:, :] = pooled_out[1:, :] * (1.0 / plan.slot_area)
    part = split_dot(pooled_out[...], w_squeeze[...])
    squeeze_send[...] = part
    swap = partner(squeeze_send, squeeze_recv, base + 3)
    swap.wait()
    squeeze_pre = part + squeeze_recv[...] + vec[SQUEEZE_BIAS : SQUEEZE_BIAS + 1, :group]
    squeeze_pre_out[...] = squeeze_pre
    squeezed = squeeze_pre * sigmoid(squeeze_pre)
    excite_out[...] = sigmoid(
        split_dot(squeezed, w_excite[...]) + vec[EXCITE_BIAS : EXCITE_BIAS + 1, :]
    )

    def activate_three(start, place, crop, carry):
        act_three[core, pl.ds(start, TILE), :] = (
            act_two[pl.ds(start, TILE), :] * excite_out[pl.ds(crop, 1), :]
        ).astype(BF16)
        return carry

    plan.sweep(activate_three, 0)
    exchange = partner(act_three.at[core], act_three.at[core], base + 4)
    exchange.wait()
    saves.append(local(act_three, act_three_out, base + 9))
    for copy in others + saves:
        copy.wait()


def forward(plan, x_own, w_in, w_mid, k_out, vec, vec_three, mask, w_squeeze, w_excite):
    n, half, group = plan.dp, plan.half, plan.group
    shape = jax.ShapeDtypeStruct
    copies = 1 + plan.slots
    pay = 2 * half + LANE
    return pl.pallas_call(
        functools.partial(forward_kernel, plan),
        out_shape=(
            shape((2, plan.all, half), BF16),
            shape((plan.all, half), F32),
            shape((plan.conv, half), BF16),
            shape((plan.conv, half), F32),
            shape((2, plan.all, half), BF16),
            shape((2,) + k_out.shape, BF16),
            shape((2,) + w_in.shape, BF16),
            shape((2,) + vec_three.shape, F32),
            shape((8, half), F32),
            shape((plan.slot_rows, half), F32),
            shape((plan.slot_rows, half), F32),
            shape((plan.slot_rows, group), F32),
        ),
        in_specs=[ANY, VMEM, ANY, ANY, ANY, VMEM, ANY, VMEM, VMEM, VMEM],
        out_specs=(ANY,) * 8 + (VMEM,) * 4,
        scratch_shapes=[
            pltpu.VMEM((2, plan.all, half), BF16),
            pltpu.VMEM((plan.all, half), F32),
            pltpu.VMEM((2, plan.conv, 3 * group), BF16),
            pltpu.VMEM(w_mid.shape, BF16),
            pltpu.VMEM((plan.conv, half), F32),
            pltpu.VMEM((plan.all, half), F32),
            pltpu.VMEM((2, plan.all, half), BF16),
            pltpu.VMEM((1, pay), F32),
            pltpu.VMEM((n, 1, pay), F32),
            pltpu.VMEM((1, pay), F32),
            pltpu.VMEM((n, 1, pay), F32),
            pltpu.VMEM((plan.slot_rows, group), F32),
            pltpu.VMEM((plan.slot_rows, group), F32),
            pltpu.SemaphoreType.DMA((copies + 10,)),
            pltpu.SemaphoreType.DMA((copies + 5,)),
            pltpu.SemaphoreType.DMA((copies + 5,)),
            pltpu.SemaphoreType.DMA((2, n)),
            pltpu.SemaphoreType.DMA((2, n)),
        ],
        compiler_params=pltpu.CompilerParams(
            collective_id=0, has_side_effects=True, vmem_limit_bytes=VMEM_BYTES
        ),
    )(x_own, w_in, w_mid, k_out, w_in, vec, vec_three, mask, w_squeeze, w_excite)


def halves(rows, plan):
    real = plan.half_real
    pad = ((0, 0), (0, plan.half - real))
    return jnp.stack([jnp.pad(rows[:, :real], pad), jnp.pad(rows[:, real:], pad)], 0)


def own_rows(glob, small, plan):
    glob = jnp.pad(glob[0], ((0, 0), (0, plan.glob_width - plan.glob_side), (0, 0)))
    small = jnp.pad(small, ((0, 0), (0, 0), (0, plan.small_width - plan.small_side), (0, 0)))
    return halves(
        jnp.concatenate(
            [glob.reshape(-1, plan.channels), small.reshape(-1, plan.channels)], 0
        ),
        plan,
    )


def group_lanes(array, plan):
    pad = ((0, 0),) * (array.ndim - 1) + ((0, plan.group - plan.width),)
    return jnp.concatenate(
        [jnp.pad(array[..., : plan.width], pad), jnp.pad(array[..., plan.width :], pad)], -1
    )


def group_rows(array, plan):
    pieces = array.reshape(-1, plan.width, array.shape[1])
    pieces = jnp.pad(pieces, ((0, 0), (0, plan.group - plan.width), (0, 0)))
    return pieces.reshape(-1, array.shape[1])


def pad_to(array, *sizes):
    return jnp.pad(array, [(0, size - have) for size, have in zip(sizes, array.shape)])


def row_masks(plan, small_count):
    glob = (lax.iota(jnp.int32, plan.glob_width) < plan.glob_side).astype(F32)
    small = (lax.iota(jnp.int32, plan.small_width) < plan.small_side).astype(F32)
    live = (lax.iota(jnp.int32, plan.slots) < small_count[0]).astype(F32)

    def build(times):
        first = jnp.tile(glob, times * plan.glob_height)
        rest = (live[:, None] * jnp.tile(small, times * plan.small_height)[None]).reshape(-1)
        return jnp.broadcast_to(jnp.concatenate([first, rest])[:, None], (first.size + rest.size, LANE))

    count = plan.glob_area + plan.slot_area * small_count[0].astype(F32)
    return build(2), build(1), count
def prepare(
    dp,
    glob_in,
    small_in,
    small_count,
    kernel_in,
    kernel_mid,
    kernel_out,
    squeeze_weight,
    squeeze_bias,
    excite_weight,
    excite_bias,
    gain_first,
    shift_first,
    gain_second,
    shift_second,
    gain_third,
    shift_third,
    glob_cotangent,
    small_cotangent,
):
    plan = Plan(glob_in.shape, small_in.shape, kernel_mid.shape[2], dp)
    half, group, real = plan.half, plan.group, plan.half_real
    x_own = own_rows(glob_in, small_in, plan)
    cot_own = own_rows(glob_cotangent, small_cotangent, plan)
    w_in = group_lanes(kernel_in, plan)
    w_in = jnp.stack([pad_to(w_in[:real], half, half), pad_to(w_in[real:], half, half)], 0)
    w_mid = pad_to(group_lanes(kernel_mid, plan), 3, 3, group, half).reshape(3, 3 * group, half)
    k_out = group_rows(pad_to(kernel_out, plan.channels, half), plan).reshape(2, half, half)
    w_squeeze = group_rows(pad_to(squeeze_weight, real, group), plan)
    w_excite = pad_to(group_lanes(excite_weight, plan), group, half)
    mask_all, mask_own, count = row_masks(plan, small_count)

    def grouped(vector):
        return group_lanes(vector.astype(F32)[None], plan)

    vec = jnp.concatenate(
        [
            grouped(gain_first),
            grouped(shift_first),
            grouped(gain_second),
            grouped(shift_second),
            grouped(excite_bias),
            pad_to(squeeze_bias.astype(F32)[None], 1, half),
            jnp.full((1, half), count, F32),
            jnp.zeros((1, half), F32),
        ],
        0,
    )
    vec_three = pad_to(jnp.stack([gain_third, shift_third], 0).astype(F32), 8, half)
    return plan, x_own, cot_own, w_in, w_mid, k_out, w_squeeze, w_excite, mask_all, mask_own, vec, vec_three
def own_steps(plan, body, carry):
    step = 32

    def run(tile, state):
        return body(pl.multiple_of(tile * step, step), step, state)

    return lax.fori_loop(0, plan.own // step, run, carry)


def merge_two(first, second, lanes):
    sums = [part[:, :lanes] for part in (first, second)]
    squares = [part[:, lanes : 2 * lanes] for part in (first, second)]
    counts = [widen(part[:, 2 * lanes :], lanes) for part in (first, second)]
    total = sums[0] + sums[1]
    count = counts[0] + counts[1]
    mean = total / count
    spread = squares[0] + squares[1]
    for index in range(2):
        gap = sums[index] / counts[index] - mean
        spread = spread + counts[index] * gap * gap
    return total, spread, count


def third_kernel(
    plan,
    act_three_hbm,
    k_out_hbm,
    x_own,
    cot_own,
    mask,
    vec,
    vec_three,
    result_out,
    grad_summed_out,
    grad_pre_three_out,
    sums_out,
    act_three,
    k_out,
    pre_three,
    grad_summed,
    grad_pre_three,
    pay,
    pair,
    chip,
    slots,
    finals,
    pay_back,
    pair_back,
    chip_back,
    slots_back,
    finals_back,
    local_sem,
    send_sem,
    recv_sem,
    spread_send,
    spread_recv,
):
    n, half = plan.dp, plan.half
    me, core = lax.axis_index("dp"), lax.axis_index("rows")
    pieces = plan.own_pieces(core)
    entry_barrier(n, me, core)

    def local(source, target, index):
        copy = pltpu.make_async_copy(source, target, local_sem.at[index])
        copy.start()
        return copy

    def partner(source, target, index):
        copy = to_partner(me, core, source, target, send_sem.at[index], recv_sem.at[index])
        copy.start()
        return copy

    loads = [
        local(
            act_three_hbm.at[:, pl.ds(place, length), :],
            act_three.at[:, pl.ds(start, length), :],
            index,
        )
        for index, (place, start, length) in enumerate(pieces)
    ]
    base = len(pieces)
    loads.append(local(k_out_hbm, k_out, base))
    for copy in loads:
        copy.wait()
    own_count = 0.5 * vec[COUNT : COUNT + 1, :]

    block = plan.own // 2
    for side in range(2):

        def product(part, carry, side=side):
            rows = pl.ds(pl.multiple_of(part * block, 16), block)
            pre_three[side, rows, :] = dot(act_three[0, rows, :], k_out[side, 0]) + dot(
                act_three[1, rows, :], k_out[side, 1]
            )
            return carry

        lax.fori_loop(0, 2, product, 0)

    for side in range(2):

        def add(row, step, carry, side=side):
            rows = pl.ds(row, step)
            return carry + rows_down(pre_three[side, rows, :] * widen(mask[rows, :], half))

        total = jnp.sum(own_steps(plan, add, jnp.zeros((8, half), F32)), 0, keepdims=True)
        mean = total / own_count

        def spread(row, step, carry, side=side, mean=mean):
            rows = pl.ds(row, step)
            gap = (pre_three[side, rows, :] - mean) * widen(mask[rows, :], half)
            return carry + rows_down(gap * gap)

        squares = jnp.sum(own_steps(plan, spread, jnp.zeros((8, half), F32)), 0, keepdims=True)
        pay[side, :, :half] = total
        pay[side, :, half : 2 * half] = squares
        pay[side, :, 2 * half :] = own_count[:, :LANE]
    partner(pay.at[1 - core], pair, 0).wait()
    total, squares, count = merge_two(pay[core], pair[...], half)
    chip[:, :half] = total
    chip[:, half : 2 * half] = squares
    chip[:, 2 * half :] = count[:, :LANE]
    exchange = Spread(n, me, core, chip, slots, spread_send.at[0], spread_recv.at[0])
    exchange.start()
    exchange.wait()
    mean, variance, full_count = merge_moments(slots, n, half)
    finals[core, :, :half] = mean
    finals[core, :, half:] = lax.rsqrt(variance + EPSILON)
    partner(finals.at[core], finals.at[core], 1).wait()

    for side in range(2):
        mean = finals[side, :, :half]
        inverse = finals[side, :, half:]
        gain = vec_three[side, :1, :]
        shift = vec_three[side, 1:2, :]

        def outer(row, step, carry, side=side, mean=mean, inverse=inverse, gain=gain, shift=shift):
            rows = pl.ds(row, step)
            seen = widen(mask[rows, :], half)
            normed = (pre_three[side, rows, :] - mean) * inverse
            summed = normed * gain + shift + x_own[side, rows, :].astype(F32)
            sigma = sigmoid(summed)
            result_out[side, rows, :] = (seen * summed * sigma).astype(BF16)
            slope = sigma * (1.0 + summed * (1.0 - sigma))
            grad = cot_own[side, rows, :].astype(F32) * seen * slope
            grad_summed[side, rows, :] = grad
            grad_summed_out[side, rows, :] = grad.astype(BF16)
            return carry[0] + rows_down(grad), carry[1] + rows_down(grad * normed)

        zero = jnp.zeros((8, half), F32)
        shift_sum, gain_sum = own_steps(plan, outer, (zero, zero))
        pay_back[side, :, :half] = jnp.sum(shift_sum, 0, keepdims=True)
        pay_back[side, :, half:] = jnp.sum(gain_sum, 0, keepdims=True)
    partner(pay_back.at[1 - core], pair_back, 2).wait()
    chip_back[...] = pay_back[core] + pair_back[...]
    exchange = Spread(n, me, core, chip_back, slots_back, spread_send.at[1], spread_recv.at[1])
    exchange.start()
    exchange.wait()

    finals_back[core] = gather_sum(slots_back, n, 2 * half)
    partner(finals_back.at[core], finals_back.at[core], 3).wait()
    copies = []
    for side in range(2):
        mean = finals[side, :, :half]
        inverse = finals[side, :, half:]
        shift_sum = finals_back[side, :, :half]
        gain_sum = finals_back[side, :, half:]
        sums_out[side] = jnp.concatenate([shift_sum, gain_sum, jnp.zeros((6, half), F32)], 0)
        scale = vec_three[side, :1, :] * inverse
        shift_mean = shift_sum / full_count
        gain_mean = gain_sum / full_count

        def inner(
            row, step, carry, side=side, mean=mean, inverse=inverse, scale=scale,
            shift_mean=shift_mean, gain_mean=gain_mean
        ):
            rows = pl.ds(row, step)
            normed = (pre_three[side, rows, :] - mean) * inverse
            grad = scale * (grad_summed[side, rows, :] - shift_mean - normed * gain_mean)
            grad_pre_three[side, rows, :] = (grad * widen(mask[rows, :], half)).astype(BF16)
            return carry

        own_steps(plan, inner, 0)
        for index, (place, start, length) in enumerate(pieces):
            source = grad_pre_three.at[side, pl.ds(start, length), :]
            target = grad_pre_three_out.at[side, pl.ds(place, length), :]
            copies.append(partner(source, target, 4 + side * base + index))
            copies.append(local(source, target, base + 1 + side * base + index))
    for copy in copies:
        copy.wait()


def gather_sum(slots, n, lanes):
    def add(step, carry):
        return carry + slots[step]

    return lax.fori_loop(0, n, add, jnp.zeros((1, lanes), F32))


def third(plan, act_three, k_out_all, x_own, cot_own, mask, vec, vec_three):
    n, half = plan.dp, plan.half
    shape = jax.ShapeDtypeStruct
    pieces = 1 + plan.slots
    pay = 2 * half + LANE
    own = (2, plan.own, half)
    return pl.pallas_call(
        functools.partial(third_kernel, plan),
        out_shape=(
            shape(own, BF16),
            shape(own, BF16),
            shape((2, plan.all, half), BF16),
            shape((2, 8, half), F32),
        ),
        in_specs=[ANY, ANY, VMEM, VMEM, VMEM, VMEM, VMEM],
        out_specs=(VMEM, VMEM, ANY, VMEM),
        scratch_shapes=[
            pltpu.VMEM(own, BF16),
            pltpu.VMEM(k_out_all.shape, BF16),
            pltpu.VMEM(own, F32),
            pltpu.VMEM(own, F32),
            pltpu.VMEM(own, BF16),
            pltpu.VMEM((2, 1, pay), F32),
            pltpu.VMEM((1, pay), F32),
            pltpu.VMEM((1, pay), F32),
            pltpu.VMEM((n, 1, pay), F32),
            pltpu.VMEM((2, 1, 2 * half), F32),
            pltpu.VMEM((2, 1, 2 * half), F32),
            pltpu.VMEM((1, 2 * half), F32),
            pltpu.VMEM((1, 2 * half), F32),
            pltpu.VMEM((n, 1, 2 * half), F32),
            pltpu.VMEM((2, 1, 2 * half), F32),
            pltpu.SemaphoreType.DMA((3 * pieces + 1,)),
            pltpu.SemaphoreType.DMA((2 * pieces + 4,)),
            pltpu.SemaphoreType.DMA((2 * pieces + 4,)),
            pltpu.SemaphoreType.DMA((2, n)),
            pltpu.SemaphoreType.DMA((2, n)),
        ],
        compiler_params=pltpu.CompilerParams(
            collective_id=1, has_side_effects=True, vmem_limit_bytes=VMEM_BYTES
        ),
    )(act_three, k_out_all, x_own, cot_own, mask, vec, vec_three)


class Steps:
    def __init__(self, n, me, core):
        bits = n.bit_length() - 1
        self.halvings = min(bits, 4)
        self.shards = 2**self.halvings
        self.doublings = bits - self.halvings
        self.bit, self.partner = [], []
        for step in range(bits):
            first, second = 2**step, 2 ** (step + 1 - 2 * (step % 2))
            if step >= 2 or bits < 2:
                second = first
            distance = first + (second - first) * core
            bit = lax.rem(me // distance, 2)
            self.bit.append(bit)
            self.partner.append((me + distance * (1 - 2 * bit), core))


class Reduction:
    def __init__(self, steps, rows, work, land, gathered, send, recv, local):
        self.steps, self.rows = steps, rows
        self.work, self.land, self.gathered = work, land, gathered
        self.send, self.recv, self.local = send, recv, local
        self.shard = rows // steps.shards
        self.step = 0
        self.at = 0
        self.pending = None
        self.sending = True

    def remote(self, source, target, step):
        return pltpu.make_async_remote_copy(
            src_ref=source,
            dst_ref=target,
            send_sem=self.send.at[self.slot],
            recv_sem=self.recv.at[self.slot],
            device_id=self.steps.partner[step],
            device_id_type=MESH,
        )

    def reduce_last(self):
        return self.steps.halvings + self.steps.doublings

    def place(self, row):
        return row if isinstance(row, int) else pl.multiple_of(row, 16)

    def begin(self):
        step = self.step
        self.slot = step
        if step < self.steps.halvings:
            length = self.rows >> (step + 1)
            bit = self.steps.bit[step]
            self.keep = self.at + bit * length
            gone = self.at + (1 - bit) * length
            low = self.rows - 2 * length
            self.now = (self.land.at[pl.ds(low, length), :], length)
            source = self.work.at[pl.ds(self.place(gone), length), :]
            self.pending = self.remote(source, self.now[0], step)
        else:
            low = self.rows - self.shard + (step - self.steps.halvings) * self.shard
            self.keep = self.at
            self.now = (self.land.at[pl.ds(low, self.shard), :], self.shard)
            source = self.work.at[pl.ds(self.place(self.at), self.shard), :]
            self.pending = self.remote(source, self.now[0], step)
        self.pending.start()

    def end(self):
        self.pending.wait()
        self.pending = None
        landed, length = self.now
        size = 48 if self.shard % 48 == 0 else 16

        def add(tile, carry):
            there = pl.ds(self.place(self.keep + tile * size), size)
            here = pl.ds(pl.multiple_of(tile * size, 16), size)
            total = self.work[there, :].astype(F32) + landed[here, :].astype(F32)
            self.work[there, :] = total.astype(BF16)
            return carry

        lax.fori_loop(0, length // size, add, 0)
        self.at = self.keep
        self.step += 1

    def advance(self):
        if self.pending is not None:
            self.end()
        if self.step < self.reduce_last():
            self.begin()

    def reduced(self):
        return self.step == self.reduce_last()


class Gathering:
    def __init__(self, steps, rows, at, shard_ref, gathered, send, recv, local):
        self.steps, self.rows = steps, rows
        self.at, self.shard_ref, self.gathered = at, shard_ref, gathered
        self.send, self.recv, self.local = send, recv, local
        self.shard = rows // steps.shards
        self.step = steps.halvings - 1
        self.length = self.shard
        self.pending = None
        self.first = None

    def advance(self):
        if self.pending is not None:
            self.pending.wait()
            self.pending = None
            self.at = self.at - self.steps.bit[self.step] * self.length
            self.length *= 2
            self.step -= 1
        if self.step >= 0:
            rows = pl.ds(pl.multiple_of(self.at, 16), self.length)
            target = self.gathered.at[rows, :]
            if self.first is None:
                self.first = pltpu.make_async_copy(self.shard_ref, target, self.local)
                self.first.start()
                self.first.wait()
                source = self.shard_ref
            else:
                source = target
            self.pending = pltpu.make_async_remote_copy(
                src_ref=source,
                dst_ref=target,
                send_sem=self.send.at[self.step],
                recv_sem=self.recv.at[self.step],
                device_id=self.steps.partner[self.step],
                device_id_type=MESH,
            )
            self.pending.start()

    def done(self):
        return self.step < 0 and self.pending is None


def shard_place(steps, rows):
    place = 0
    for step in range(steps.halvings):
        place = place + steps.bit[step] * (rows >> (step + 1))
    return place


def land_rows(n, rows):
    bits = n.bit_length() - 1
    halvings = min(bits, 4)
    shard = rows >> halvings
    return rows - shard + max(bits - halvings, 0) * shard


def silu_slope(value, sigma):
    return sigma * (1.0 + value * (1.0 - sigma))
SHIFT_TWO_SUM, GAIN_TWO_SUM, EXCITE_SUM, SQUEEZE_SUM = range(4)
SHIFT_ONE_SUM, GAIN_ONE_SUM = range(2)


def second_kernel(
    plan,
    grad_pre_three_hbm,
    act_three_hbm,
    k_out_hbm,
    pre_two_hbm,
    stats,
    vec,
    mask,
    pooled,
    excite,
    squeeze_pre,
    w_squeeze,
    w_excite,
    shard_out,
    grad_norm_out,
    grad_excite_out,
    grad_squeeze_out,
    sums_out,
    grad_pre_three,
    act_three,
    k_out,
    pre_two,
    grad_act,
    slopes,
    work,
    land,
    grad_excite,
    squeeze_send,
    squeeze_recv,
    grad_pooled,
    factors,
    factor_slots,
    pay,
    slots,
    local_sem,
    pair_send,
    pair_recv,
    spread_send,
    spread_recv,
    reduce_send,
    reduce_recv,
):
    n, half, group = plan.dp, plan.half, plan.group
    me, core = lax.axis_index("dp"), lax.axis_index("rows")
    entry_barrier(n, me, core)

    def local(source, target, index):
        copy = pltpu.make_async_copy(source, target, local_sem.at[index])
        copy.start()
        return copy

    loads = [
        local(grad_pre_three_hbm, grad_pre_three, 0),
        local(act_three_hbm, act_three, 1),
        local(k_out_hbm.at[:, core], k_out, 2),
        local(pre_two_hbm, pre_two, 3),
    ]
    loads[0].wait()
    loads[1].wait()
    for side in range(2):
        for part in range(2):
            lanes = slice(part * group, (part + 1) * group)
            low = side * half + part * group
            work[low : low + group, :] = dot_tn(
                act_three[side, :, lanes], grad_pre_three[core]
            ).astype(BF16)
    steps = Steps(n, me, core)
    reduction = Reduction(steps, 2 * half, work, land, None, reduce_send, reduce_recv, None)
    reduction.advance()
    loads[2].wait()

    block = plan.all // 4

    def product(part, carry):
        rows = pl.ds(pl.multiple_of(part * block, 16), block)
        grad_act[rows, :] = dot_nt(grad_pre_three[0, rows, :], k_out[0]) + dot_nt(
            grad_pre_three[1, rows, :], k_out[1]
        )
        return carry

    lax.fori_loop(0, 4, product, 0)
    loads[3].wait()
    reduction.advance()

    mean = stats[MEAN_TWO : MEAN_TWO + 1, :]
    inverse = stats[INVERSE_TWO : INVERSE_TWO + 1, :]
    count = stats[TOTAL : TOTAL + 1, :]
    gain = vec[GAIN_TWO : GAIN_TWO + 1, :]
    shift = vec[SHIFT_TWO : SHIFT_TWO + 1, :]
    grad_excite[...] = jnp.zeros_like(grad_excite)

    def excitation(start, place, crop, carry):
        rows = pl.ds(start, TILE)
        norm = (pre_two[pl.ds(place, TILE), :] - mean) * (inverse * gain) + shift
        sigma = sigmoid(norm)
        seen = widen(mask[rows, :], half)
        slopes[rows, :] = silu_slope(norm, sigma) * seen
        term = grad_act[rows, :] * (norm * sigma * seen)
        grad_excite[pl.ds(crop, 1), :] += jnp.sum(term, 0, keepdims=True)
        return carry

    plan.sweep(excitation, 0)
    level = excite[...]
    grad_excite_pre = grad_excite[...] * level * (1.0 - level)
    part = split_dot(grad_excite_pre, w_excite[...], nt=True)
    squeeze_send[...] = part
    swap = to_partner(me, core, squeeze_send, squeeze_recv, pair_send.at[0], pair_recv.at[0])
    swap.start()
    reduction.advance()
    swap.wait()
    before = squeeze_pre[...]
    sigma = sigmoid(before)
    squeezed = before * sigma
    grad_squeeze_pre = (part + squeeze_recv[...]) * silu_slope(before, sigma)
    back = split_dot(grad_squeeze_pre, w_squeeze[...], nt=True)
    crop_row = lax.broadcasted_iota(jnp.int32, back.shape, 0)
    area = jnp.where(crop_row == 0, 1.0 / plan.glob_area, 1.0 / plan.slot_area)
    grad_pooled[...] = back * area
    deep = plan.slot_rows
    factors[:deep, :group] = squeezed.astype(BF16)
    factors[:deep, group:] = grad_excite_pre.astype(BF16)
    factors[deep:, :group] = grad_squeeze_pre.astype(BF16)
    factors[deep:, group:] = pooled[...].astype(BF16)
    factor_spread = Spread(n, me, core, factors, factor_slots, spread_send.at[0], spread_recv.at[0])
    factor_spread.start()

    def gradient(start, place, crop, carry):
        rows = pl.ds(start, TILE)
        incoming = grad_act[rows, :] * excite[pl.ds(crop, 1), :] + grad_pooled[pl.ds(crop, 1), :]
        grad = incoming * slopes[rows, :]
        grad_act[rows, :] = grad
        normed = (pre_two[pl.ds(place, TILE), :] - mean) * inverse
        return carry[0] + rows_down(grad), carry[1] + rows_down(grad * normed)

    zero = jnp.zeros((8, half), F32)
    shift_sum, gain_sum = plan.sweep(gradient, (zero, zero))
    save = local(grad_act, grad_norm_out, 4)
    pay[:, :half] = jnp.sum(shift_sum, 0, keepdims=True)
    pay[:, half:] = jnp.sum(gain_sum, 0, keepdims=True)
    spread = Spread(n, me, core, pay, slots, spread_send.at[1], spread_recv.at[1])
    spread.start()
    while not reduction.reduced():
        reduction.advance()
    shard = reduction.shard
    store = local(work.at[pl.ds(pl.multiple_of(reduction.at, 16), shard), :], shard_out, 5)
    factor_spread.wait()
    left = factor_slots[:, :, :group].reshape(n * 2 * deep, group)
    right = factor_slots[:, :, group:].reshape(n * 2 * deep, half)
    upper = lax.broadcasted_iota(jnp.int32, left.shape, 0) % (2 * deep) < deep
    zeros = jnp.zeros_like(left)
    excite_left = jnp.where(upper, left, zeros)
    squeeze_left = jnp.where(upper, zeros, left)
    grad_excite_out[...] = dot_tn(excite_left, right)
    grad_squeeze_out[...] = dot_tn(right, squeeze_left)
    wide_upper = lax.broadcasted_iota(jnp.int32, right.shape, 0) % (2 * deep) < deep
    excite_bias = jnp.sum(jnp.where(wide_upper, right.astype(F32), 0.0), 0, keepdims=True)
    squeeze_bias = jnp.sum(squeeze_left.astype(F32), 0, keepdims=True)
    spread.wait()
    totals = gather_sum(slots, n, 2 * half)
    sums_out[...] = jnp.zeros_like(sums_out)
    sums_out[SHIFT_TWO_SUM : SHIFT_TWO_SUM + 1, :] = totals[:, :half]
    sums_out[GAIN_TWO_SUM : GAIN_TWO_SUM + 1, :] = totals[:, half:]
    sums_out[EXCITE_SUM : EXCITE_SUM + 1, :] = excite_bias
    sums_out[SQUEEZE_SUM : SQUEEZE_SUM + 1, :group] = squeeze_bias
    save.wait()
    store.wait()


def second(
    plan, grad_pre_three, act_three, k_out_all, pre_two, stats, vec, mask, pooled, excite,
    squeeze_pre, w_squeeze, w_excite
):
    n, half, group = plan.dp, plan.half, plan.group
    shape = jax.ShapeDtypeStruct
    rows = 2 * half
    shard = rows >> min(n.bit_length() - 1, 4)
    deep = plan.slot_rows
    bits = n.bit_length() - 1
    return pl.pallas_call(
        functools.partial(second_kernel, plan),
        out_shape=(
            shape((shard, half), BF16),
            shape((plan.all, half), F32),
            shape((group, half), F32),
            shape((half, group), F32),
            shape((8, half), F32),
        ),
        in_specs=[ANY] * 4 + [VMEM] * 8,
        out_specs=(ANY, ANY, VMEM, VMEM, VMEM),
        scratch_shapes=[
            pltpu.VMEM((2, plan.all, half), BF16),
            pltpu.VMEM((2, plan.all, half), BF16),
            pltpu.VMEM((2, half, half), BF16),
            pltpu.VMEM((plan.conv, half), F32),
            pltpu.VMEM((plan.all, half), F32),
            pltpu.VMEM((plan.all, half), F32),
            pltpu.VMEM((rows, half), BF16),
            pltpu.VMEM((land_rows(n, rows), half), BF16),
            pltpu.VMEM((deep, half), F32),
            pltpu.VMEM((deep, group), F32),
            pltpu.VMEM((deep, group), F32),
            pltpu.VMEM((deep, half), F32),
            pltpu.VMEM((2 * deep, group + half), BF16),
            pltpu.VMEM((n, 2 * deep, group + half), BF16),
            pltpu.VMEM((1, 2 * half), F32),
            pltpu.VMEM((n, 1, 2 * half), F32),
            pltpu.SemaphoreType.DMA((6,)),
            pltpu.SemaphoreType.DMA((1,)),
            pltpu.SemaphoreType.DMA((1,)),
            pltpu.SemaphoreType.DMA((2, n)),
            pltpu.SemaphoreType.DMA((2, n)),
            pltpu.SemaphoreType.DMA((bits,)),
            pltpu.SemaphoreType.DMA((bits,)),
        ],
        compiler_params=pltpu.CompilerParams(
            collective_id=2, has_side_effects=True, vmem_limit_bytes=VMEM_BYTES
        ),
    )(
        grad_pre_three, act_three, k_out_all, pre_two, stats, vec, mask, pooled, excite,
        squeeze_pre, w_squeeze, w_excite
    )


def first_kernel(
    plan,
    shard_out_hbm,
    grad_norm_hbm,
    pre_two_hbm,
    pre_one_hbm,
    act_one_hbm,
    x_hbm,
    w_mid_hbm,
    w_in_hbm,
    stats,
    vec,
    sums_two,
    mask,
    gathered_out,
    gathered_mid,
    gathered_in,
    grad_inputs_out,
    sums_out,
    flat,
    conv_rows,
    shifted,
    act_one,
    w_mid,
    grad_pre_one,
    grad_other,
    w_in,
    shard_out,
    work_mid,
    land_mid,
    work_in,
    land_in,
    pay,
    slots,
    local_sem,
    pair_send,
    pair_recv,
    spread_send,
    spread_recv,
    reduce_send,
    reduce_recv,
    gather_send,
    gather_recv,
):
    n, half, group = plan.dp, plan.half, plan.group
    me, core = lax.axis_index("dp"), lax.axis_index("rows")
    entry_barrier(n, me, core)

    def local(source, target, index):
        copy = pltpu.make_async_copy(source, target, local_sem.at[index])
        copy.start()
        return copy

    load_norm = local(grad_norm_hbm, flat, 0)
    load_two = local(pre_two_hbm, conv_rows, 1)
    load_shard = local(shard_out_hbm, shard_out, 2)
    load_act = local(act_one_hbm, act_one, 3)
    load_mid = local(w_mid_hbm, w_mid, 4)
    load_in = local(w_in_hbm, w_in, 5)
    steps = Steps(n, me, core)
    rows_out = gathered_out.shape[0]
    load_shard.wait()
    chains = [
        Gathering(
            steps,
            rows_out,
            shard_place(steps, rows_out),
            shard_out,
            gathered_out,
            gather_send.at[0],
            gather_recv.at[0],
            local_sem.at[6],
        )
    ]
    chains[0].advance()
    for side in range(2):
        shifted[side, : plan.glob_base, :] = jnp.zeros((plan.glob_base, 3 * group), BF16)
        shifted[side, plan.glob_base + plan.glob_all : plan.small_base, :] = jnp.zeros(
            (plan.glob_width, 3 * group), BF16
        )
        for slot in range(plan.slots):
            low = plan.small_base + slot * plan.slot_conv + plan.slot_all
            shifted[side, low : low + plan.small_width, :] = jnp.zeros(
                (plan.small_width, 3 * group), BF16
            )
    mean = stats[MEAN_TWO : MEAN_TWO + 1, :]
    inverse = stats[INVERSE_TWO : INVERSE_TWO + 1, :]
    count = stats[TOTAL : TOTAL + 1, :]
    scale = vec[GAIN_TWO : GAIN_TWO + 1, :] * inverse
    shift_mean = sums_two[SHIFT_TWO_SUM : SHIFT_TWO_SUM + 1, :] / count
    gain_mean = sums_two[GAIN_TWO_SUM : GAIN_TWO_SUM + 1, :] / count * inverse
    load_norm.wait()
    load_two.wait()

    def into_two(start, place, crop, carry):
        rows = pl.ds(start, TILE)
        centered = conv_rows[pl.ds(place, TILE), :] - mean
        grad = scale * (flat[rows, :] - shift_mean - centered * gain_mean)
        grad = grad * widen(mask[rows, :], half)
        after = pltpu.roll(grad, TILE - 1, 0)
        before = pltpu.roll(grad, 1, 0)
        for tap, value in enumerate((after, grad, before)):
            for side in range(2):
                shifted[side, pl.ds(place, TILE), tap * group : (tap + 1) * group] = value[
                    :, side * group : (side + 1) * group
                ].astype(BF16)
        return carry

    plan.sweep(into_two, 0)
    load_one = local(pre_one_hbm, flat, 0)
    load_act.wait()
    chains[0].advance()

    def advance_all():
        for index, chain in enumerate(chains):
            if isinstance(chain, Reduction) and chain.reduced():
                place = pl.ds(pl.multiple_of(chain.at, 16), chain.shard)
                chains[index] = Gathering(
                    steps,
                    chain.rows,
                    chain.at,
                    chain.work.at[place, :],
                    chain.gathered,
                    gather_send.at[index],
                    gather_recv.at[index],
                    local_sem.at[6 + index],
                )
            chains[index].advance()

    for tap in range(3):
        for side in range(2):
            lanes = slice(side * group, (side + 1) * group)
            total = None
            for low, length, width in plan.segments():
                first = low - (tap - 1) * width
                term = dot_tn(
                    act_one[low : low + length, lanes], shifted[side, first : first + length, :]
                )
                total = term if total is None else total + term
            work_mid[tap, lanes, :] = total.astype(BF16)
        chains.append(
            Reduction(
                steps,
                half,
                work_mid.at[tap],
                land_mid.at[tap],
                gathered_mid.at[tap],
                reduce_send.at[tap],
                reduce_recv.at[tap],
                None,
            )
        )
        advance_all()
    load_mid.wait()

    for low, length, width in plan.segments():
        block = length // 2
        for side in range(2):
            lanes = slice(side * group, (side + 1) * group)
            for part in range(2):
                at = low + part * block
                total = None
                for tap in range(3):
                    first = at - (tap - 1) * width
                    for column in range(3):
                        taps = slice(column * group, (column + 1) * group)
                        term = dot_nt(
                            shifted[side, first : first + block, taps], w_mid[tap, taps, lanes]
                        )
                        total = term if total is None else total + term
                conv_rows[at : at + block, lanes] = total
        advance_all()
    load_x = local(x_hbm, shifted.at[:, pl.ds(0, plan.all), pl.ds(0, half)], 1)
    load_one.wait()

    mean = stats[MEAN_ONE : MEAN_ONE + 1, :]
    inverse = stats[INVERSE_ONE : INVERSE_ONE + 1, :]
    gain = vec[GAIN_ONE : GAIN_ONE + 1, :]
    shift = vec[SHIFT_ONE : SHIFT_ONE + 1, :]

    def gradient(start, place, crop, carry):
        rows = pl.ds(start, TILE)
        normed = (flat[rows, :] - mean) * inverse
        norm = normed * gain + shift
        sigma = sigmoid(norm)
        grad = conv_rows[pl.ds(place, TILE), :] * silu_slope(norm, sigma)
        grad = grad * widen(mask[rows, :], half)
        conv_rows[pl.ds(place, TILE), :] = grad
        return carry[0] + rows_down(grad), carry[1] + rows_down(grad * normed)

    zero = jnp.zeros((8, half), F32)
    shift_sum, gain_sum = plan.sweep(gradient, (zero, zero))
    pay[:, :half] = jnp.sum(shift_sum, 0, keepdims=True)
    pay[:, half:] = jnp.sum(gain_sum, 0, keepdims=True)
    spread = Spread(n, me, core, pay, slots, spread_send, spread_recv)
    spread.start()
    advance_all()
    spread.wait()
    totals = gather_sum(slots, n, 2 * half)
    sums_out[...] = jnp.zeros_like(sums_out)
    sums_out[SHIFT_ONE_SUM : SHIFT_ONE_SUM + 1, :] = totals[:, :half]
    sums_out[GAIN_ONE_SUM : GAIN_ONE_SUM + 1, :] = totals[:, half:]
    scale = gain * inverse
    shift_mean = totals[:, :half] / count
    gain_mean = totals[:, half:] / count * inverse

    def into_one(start, place, crop, carry):
        rows = pl.ds(start, TILE)
        centered = flat[rows, :] - mean
        grad = scale * (conv_rows[pl.ds(place, TILE), :] - shift_mean - centered * gain_mean)
        grad_pre_one[rows, :] = (grad * widen(mask[rows, :], half)).astype(BF16)
        return carry

    plan.sweep(into_one, 0)
    swaps = []
    for index, (place, start, length) in enumerate(plan.own_pieces(1 - core)):
        swap = to_partner(
            me,
            core,
            grad_pre_one.at[pl.ds(place, length), :],
            grad_other.at[pl.ds(start, length), :],
            pair_send.at[index],
            pair_recv.at[index],
        )
        swap.start()
        swaps.append(swap)
    load_x.wait()
    for side in range(2):
        for part in range(2):
            lanes = slice(part * group, (part + 1) * group)
            low = side * half + part * group
            work_in[low : low + group, :] = dot_tn(
                shifted[side, : plan.all, lanes], grad_pre_one[...]
            ).astype(BF16)
    chains.append(
        Reduction(
            steps, 2 * half, work_in, land_in, gathered_in, reduce_send.at[3], reduce_recv.at[3], None
        )
    )
    advance_all()
    load_in.wait()
    for swap in swaps:
        swap.wait()
    pieces = plan.own_pieces(core)
    own = [
        grad_pre_one[pl.ds(pieces[0][0], plan.glob_own), :],
        jnp.concatenate([grad_pre_one[pl.ds(spot, size), :] for spot, _, size in pieces[1:]], 0),
    ]
    marks = (0, plan.glob_own, plan.own)
    for part in range(2):
        rows = slice(marks[part], marks[part + 1])
        for side in range(2):
            grad_inputs_out[side, rows, :] = (
                dot_nt(own[part], w_in[core, side])
                + dot_nt(grad_other[rows, :], w_in[1 - core, side])
            ).astype(BF16)
        advance_all()
    while not all(isinstance(chain, Gathering) and chain.done() for chain in chains):
        advance_all()


def first(
    plan, shard_out, grad_norm, pre_two, pre_one, act_one, x_all, w_mid, w_in_all, stats, vec,
    sums_two, mask
):
    n, half, group = plan.dp, plan.half, plan.group
    shape = jax.ShapeDtypeStruct
    bits = n.bit_length() - 1
    pieces = 1 + plan.slots
    return pl.pallas_call(
        functools.partial(first_kernel, plan),
        out_shape=(
            shape((2 * half, half), BF16),
            shape((3, half, 3 * group), BF16),
            shape((2 * half, half), BF16),
            shape((2, plan.own, half), BF16),
            shape((8, half), F32),
        ),
        in_specs=[ANY] * 8 + [VMEM] * 4,
        out_specs=(ANY, ANY, ANY, VMEM, VMEM),
        scratch_shapes=[
            pltpu.VMEM((plan.all, half), F32),
            pltpu.VMEM((plan.conv, half), F32),
            pltpu.VMEM((2, plan.conv, 3 * group), BF16),
            pltpu.VMEM((plan.conv, half), BF16),
            pltpu.VMEM(w_mid.shape, BF16),
            pltpu.VMEM((plan.all, half), BF16),
            pltpu.VMEM((plan.own, half), BF16),
            pltpu.VMEM(w_in_all.shape, BF16),
            pltpu.VMEM(shard_out.shape, BF16),
            pltpu.VMEM((3, half, 3 * group), BF16),
            pltpu.VMEM((3, land_rows(n, half), 3 * group), BF16),
            pltpu.VMEM((2 * half, half), BF16),
            pltpu.VMEM((land_rows(n, 2 * half), half), BF16),
            pltpu.VMEM((1, 2 * half), F32),
            pltpu.VMEM((n, 1, 2 * half), F32),
            pltpu.SemaphoreType.DMA((11,)),
            pltpu.SemaphoreType.DMA((pieces,)),
            pltpu.SemaphoreType.DMA((pieces,)),
            pltpu.SemaphoreType.DMA((n,)),
            pltpu.SemaphoreType.DMA((n,)),
            pltpu.SemaphoreType.DMA((4, bits)),
            pltpu.SemaphoreType.DMA((4, bits)),
            pltpu.SemaphoreType.DMA((5, 4)),
            pltpu.SemaphoreType.DMA((5, 4)),
        ],
        compiler_params=pltpu.CompilerParams(
            collective_id=3, has_side_effects=True, vmem_limit_bytes=VMEM_BYTES
        ),
    )(
        shard_out, grad_norm, pre_two, pre_one, act_one, x_all, w_mid, w_in_all, stats, vec,
        sums_two, mask
    )


def pixels(rows, plan):
    glob = rows[:, : plan.glob_own].reshape(2, plan.glob_height, plan.glob_width, plan.half)
    small = rows[:, plan.glob_own :].reshape(
        2, plan.slots, plan.small_height, plan.small_width, plan.half
    )
    real = plan.half_real

    def join(maps):
        return jnp.concatenate([maps[0, ..., :real], maps[1, ..., :real]], -1)

    return join(glob[:, :, : plan.glob_side])[None], join(small[:, :, :, : plan.small_side])


def ungroup_lanes(array, plan):
    return jnp.concatenate(
        [array[..., : plan.width], array[..., plan.group : plan.group + plan.width]], -1
    )


def per_device(*arguments):
    dp = lax.axis_size("dp")
    core = lax.axis_index("rows")
    (
        plan, x_own, cot_own, w_in, w_mid, k_out, w_squeeze, w_excite, mask_all, mask_own, vec,
        vec_three
    ) = prepare(dp, *arguments)
    half, group, width, real = plan.half, plan.group, plan.width, plan.half_real
    (
        x_all, pre_one, act_one, pre_two, act_three, k_out_all, w_in_all, vec_three_all, stats,
        pooled, excite, squeeze_pre
    ) = forward(plan, x_own, w_in, w_mid, k_out, vec, vec_three, mask_all, w_squeeze, w_excite)
    result, grad_summed, grad_pre_three, sums_three = third(
        plan, act_three, k_out_all, x_own, cot_own, mask_own, vec, vec_three_all
    )
    shard_out, grad_norm, grad_excite, grad_squeeze, sums_two = second(
        plan, grad_pre_three, act_three, k_out_all, pre_two, stats, vec, mask_all, pooled, excite,
        squeeze_pre, w_squeeze, w_excite
    )
    gathered_out, gathered_mid, gathered_in, grad_inputs, sums_one = first(
        plan, shard_out, grad_norm, pre_two, pre_one, act_one, x_all, w_mid, w_in_all, stats, vec,
        sums_two, mask_all
    )
    glob_out, small_out = pixels(result.astype(F32), plan)
    glob_grad, small_grad = pixels(grad_inputs.astype(F32) + grad_summed.astype(F32), plan)
    grad_kernel_out = (
        gathered_out.reshape(4, group, half)[:, :width, :real].reshape(-1, real).astype(F32)
    )
    grad_kernel_in = ungroup_lanes(
        gathered_in.reshape(2, half, half)[:, :real].reshape(-1, half), plan
    ).astype(F32)
    mid = gathered_mid.reshape(3, 2, group, 3, group)[:, :, :width, :, :width]
    grad_kernel_mid = mid.transpose(0, 3, 2, 1, 4).reshape(3, 3, width, real).astype(F32)
    sums = lax.dynamic_index_in_dim(sums_three, core, 0, False)

    def grouped(row):
        return ungroup_lanes(row, plan)

    return (
        glob_out,
        small_out,
        glob_grad,
        small_grad,
        grad_kernel_in,
        grad_kernel_mid,
        grad_kernel_out,
        jnp.concatenate(
            [grad_squeeze[:width, :width], grad_squeeze[group : group + width, :width]], 0
        ),
        sums_two[SQUEEZE_SUM, :width],
        grouped(grad_excite[:width]),
        grouped(sums_two[EXCITE_SUM]),
        grouped(sums_one[GAIN_ONE_SUM]),
        grouped(sums_one[SHIFT_ONE_SUM]),
        grouped(sums_two[GAIN_TWO_SUM]),
        grouped(sums_two[SHIFT_TWO_SUM]),
        sums[1, :real],
        sums[0, :real],
    )


def solution(mesh):
    maps = P("dp", "rows", None, None)
    vector = P("rows")
    columns = P(None, "rows")
    taps = P(None, None, None, "rows")
    return jax.shard_map(
        per_device,
        mesh=mesh,
        in_specs=(
            maps, maps, P("dp"), columns, taps, columns, P("rows", None), P(), columns,
        )
        + (vector,) * 7
        + (maps, maps),
        out_specs=(maps,) * 4
        + (columns, taps, columns, P("rows", None), P(), columns)
        + (vector,) * 7,
        check_vma=False,
    )
```

time: 3610 us -> 647 us (0.18); the launches traced: 3560 us -> 636 us
  local copies, waits for them, and re-layouts: 1700 us -> 101 us
  blocking collectives: 1050 us -> 0 us
  Pallas kernels: 0 us -> 494 us
  other arithmetic: 355 us -> 39 us
  matrix products: 235 us -> 0 us
  waiting for transfers between devices: 187 us -> 0 us
    unnamed x307 -> x38, local copies, waits for them, and re-layouts: 723 us -> 35.7 us
    unnamed x3 -> x0, blocking collectives: 678 us -> none
    pallas_call x0 -> x4, Pallas kernels: none -> 494 us  [the longest x1 231 us: first(): pl.pallas_call(functools.partial(first_kernel, plan), out_shape=(shape((2...]
    reshape x66 -> x4, local copies, waits for them, and re-layouts: 458 us -> 15.2 us  [the longest x1 11 us: per_device(): mid = gathered_mid.reshape(3, 2, group, 3, group)[:, :, :width, :, :width]]
    psum x10 -> x0, blocking collectives: 367 us -> none  [the longest x3 122 us: norm_forward(): lax.psum(jnp.sum(pixel_mask * centered * centered, 0), ('dp', 'rows'))]
    dot_general x66 -> x0, matrix products: 235 us -> none  [the longest x18 73.3 us: group_conv_input(): jnp.einsum('mhwgo,cgo->mhwgc', window, weights, preferred_element_type=jn...]
    reshape x1 -> x0, other arithmetic: 226 us -> none  [reduce_all(): gathered = lax.all_gather(owned.astype(jnp.bfloat16), 'dp', axis=0, tiled...]
    all_gather x6 -> x0, waiting for transfers between devices: 185 us -> none  [the longest x1 185 us: reduce_all(): lax.all_gather(owned.astype(jnp.bfloat16), 'dp', axis=0, tiled=True)]
  transfers between devices with their start and end apart: 14 -> 0, of which waited for: 1 -> 0; matrix products, arithmetic and copies ran while one was open for 30% -> 0% of each run, Pallas kernels for 0% -> 0%
where the time goes in v1:
time: 647 us; the launch traced here: 636 us
  Pallas kernels  494 us (76%)
  local copies, waits for them, and re-layouts  101 us (16%)
  other arithmetic  39 us (6%)
    pallas_call x1, Pallas kernels, first(): pl.pallas_call(functools.partial(first_kernel, plan), out_shape=(shape((2...  231 us
    pallas_call x1, Pallas kernels, forward(): pl.pallas_call(functools.partial(forward_kernel, plan), out_shape=(shape(...  156 us
    pallas_call x1, Pallas kernels, second(): pl.pallas_call(functools.partial(second_kernel, plan), out_shape=(shape((...  63.9 us
    pallas_call x1, Pallas kernels, third(): pl.pallas_call(functools.partial(third_kernel, plan), out_shape=(shape(ow...  43.3 us
    unnamed x38, local copies, waits for them, and re-layouts  35.7 us

profile of v1, /device:TPU:0, one launch (start us, length us, event | category | flops | bytes accessed | tf_op | source)
XLA Modules:
  0.0 636.2 jit_solution(2049427302547078690)
XLA Ops:
  0.7 0.8 reshape.146
  1.5 0.7 reshape.147
  2.1 0.7 reshape.148
  2.8 0.7 reshape.149
  3.5 0.7 reshape.150
  4.2 0.7 slice_select_fusion.4
  6.0 0.7 broadcast_in_dim.70
  7.3 1.7 pad.156
  9.4 1.0 copy-done.8
  10.5 4.5 fusion.10
  15.1 2.8 pad_maximum_fusion.2
  19.4 1.6 pad_maximum_fusion.6.w_in.w_in_hbm
  21.3 1.3 broadcast_in_dim.73.mask
  22.6 3.4 slice.246
  26.0 2.0 slice_select_fusion
  28.6 2.8 pad.133
  31.6 0.9 pad.151
  32.8 0.9 pad.154.w_excite
  33.6 1.6 pad.134
  35.2 2.2 reshape.133
  37.5 1.6 pad.135
  39.7 155.6 %shard_map.305 = (bf16[2,1856,768]{2,1,0:T(8,128)(2,1)}, f32[1856,768]{1,0:T(8,128)}, bf16[2000,768]{1,0:T(8,128)(2,1)}, f32[2000,768]{1,0:T(8,128)}, bf16[2,185...) custom-call(bf16[2,928,768]{2,1,0:T(8,128)(2,1)} %get-tuple-element., ...), custom_call_target="tpu_custom_call" | custom-call | tf_op jit(solution)/shard_map/pallas_call | solution.py:433
  195.7 1.0 broadcast_in_dim.74.mask
  196.6 43.3 %shard_map.306 = (bf16[2,928,768]{2,1,0:T(8,128)(2,1)}, bf16[2,928,768]{2,1,0:T(8,128)(2,1)}, bf16[2,1856,768]{2,1,0:T(8,128)(2,1)}, f32[2,8,768]{2,1,0:T(8,128)}) custom-call(bf16[2,1856,768]{2,1,0:T(8,128)(2,1)} %get-tuple-element.43.act_three_hbm, bf16[2,2,768,768]{3,2,1,0:T(8,128)(2,1)} %get-tuple-element.44.k_out_hbm, ...), custom_call_target="tpu_custom_call" | custom-call | tf_op jit(solution)/shard_map/pallas_call | solution.py:778
  239.9 63.9 %shard_map.307 = (bf16[96,768]{1,0:T(8,128)(2,1)}, f32[1856,768]{1,0:T(8,128)}, f32[384,768]{1,0:T(8,128)}, f32[768,384]{1,0:T(8,128)}, f32[8,768]{1,0:T(8,128)}) custom-call(bf16[2,1856,768]{2,1,0:T(8,128)(2,1)} %get-tuple-element.47.grad_pre_three_hbm, bf16[2,1856,768]{2,1,0:T(8,128)(2,1)} %get-tuple-element.43.act_three_hbm, ...), custom_call_target="tpu_custom_call" | custom-call | tf_op jit(solution)/shard_map/pallas_call | solution.py:1148
  303.9 1.5 slice_reduce_fusion.3
  305.4 0.7 pad_maximum_fusion.15
  306.7 231.0 %shard_map.308 = (bf16[1536,768]{1,0:T(8,128)(2,1)}, bf16[3,768,1152]{2,1,0:T(8,128)(2,1)}, bf16[1536,768]{1,0:T(8,128)(2,1)}, bf16[2,928,768]{2,1,0:T(8,128)(2,1)}, f32[8,768]{1,0:T(8,128)}) custom-call(bf16[96,768]{1,0:T(8,128)(2,1)} %get-tuple-element.53.shard_out_hbm, f32[1856,768]{1,0:T(8,128)} %get-tuple-element.54.grad_norm_hbm, ...), custom_call_target="tpu_custom_call" | custom-call | tf_op jit(solution)/shard_map/pallas_call | solution.py:1462
  537.7 0.8 slice_reduce_fusion.7
  538.5 0.7 pad_maximum_fusion.13
  540.6 1.3 pad_maximum_fusion.8
  541.9 1.1 pad_maximum_fusion.7
  543.0 8.5 %copy.37 = bf16[3,768,1152]{1,2,0:T(8,128)(2,1)} copy(bf16[3,768,1152]{2,1,0:T(8,128)(2,1)} %get-tuple-element.63) | data formatting | bytes 10616832 | tf_op jit(solution)/shard_map/pallas_call | solution.py:1462
  551.6 11.0 %reshape.144 = bf16[3,2,384,3,384]{2,1,4,3,0:T(2,128)(2,1)} reshape(bf16[3,768,1152]{1,2,0:T(8,128)(2,1)} %copy.37) | data formatting | bytes 10616832 | tf_op jit(solution)/shard_map/reshape | solution.py:1558
  562.5 7.9 %convert_bitcast_fusion = f32[3,3,373,2,373]{2,3,4,1,0:T(2,128)} fusion(bf16[3,2,384,3,384]{2,1,4,3,0:T(2,128)(2,1)} %reshape.144), kind=kLoop, calls=%fused_computation.2 | loop fusion | flops 2504322 | bytes 15025932 | tf_op jit(solution)/shard_map/convert_element_type | solution.py:1559
  570.4 19.4 %copy.40 = f32[3,3,373,2,373]{4,3,2,1,0:T(2,128)} copy(f32[3,3,373,2,373]{2,3,4,1,0:T(2,128)} %convert_bitcast_fusion) | data formatting | bytes 20034576
  589.9 14.1 %reshape.153 = f32[3,3,373,746]{3,2,1,0:T(8,128)} reshape(f32[3,3,373,2,373]{4,3,2,1,0:T(2,128)} %copy.40) | data formatting | bytes 20034576
  603.9 1.8 slice.333
  605.7 1.8 reshape.143
  607.6 1.8 fusion.28
  609.4 3.1 maximum_convert_fusion
  612.6 1.2 copy-done.2
  614.7 2.2 pad_maximum_fusion.1
  617.8 3.1 broadcast_in_dim.76
  620.9 2.4 slice_convert_fusion
  623.3 5.1 reshape.152
  628.9 2.2 pad_maximum_fusion
  632.0 3.1 broadcast_in_dim.75
  (98 shorter events, 11.4 us)
Async XLA Ops:
  0.7 8.3 %copy-start.6 = (bf16[5,6,12,1492]{3,2,1,0:T(8,128)(2,1)S(1)}, bf16[5,6,12,1492]{3,2,1,0:T(8,128)(2,1)}, u32[]{:S(2)}) copy-start(bf16[5,6,12,1492]{3,2,1,0:T(8,128)(2,1)} %param.19) | copy-start | bytes 3222724
  7.3 1.9 copy-start.7
  9.0 1.4 copy-start.8
  9.2 1.3 copy-start.15
  15.0 2.8 copy-start.3
  15.1 3.3 copy-start.14
  28.6 2.8 copy-start.11
  31.4 1.1 copy-start.12
  31.6 2.0 copy-start.4
  37.5 1.6 copy-start.16
  37.5 1.6 copy-start.17
  306.7 233.8 %copy-start.10 = (f32[384,768]{1,0:T(8,128)S(1)}, f32[384,768]{1,0:T(8,128)}, u32[]{:S(2)}) copy-start(f32[384,768]{1,0:T(8,128)} %get-tuple-element.66) | copy-start | bytes 3538948
  540.5 1.4 copy-start.9
  609.4 3.1 copy-start.1
  609.4 4.3 copy-start.2
  617.8 3.1 copy-start.5
  623.3 5.1 copy-start
  632.0 3.1 copy-start.13
